TPU v7x, 32 devices: a whole 2x2x4 slice. The times are simulated.
32 devices in a mesh: bead: 8 (over z, x), space: 4 (over y, core).
Axes of the slice: x: 2, y: 2, z: 4, core: 2. Of those that a mesh axis runs over, the one named last changes fastest.
Arguments:
- positions: float32 [32, 64, 3, 128], P('bead', 'space'), may hold values from 0 to 1
- momenta: float32 [32, 64, 3, 128], P('bead', 'space'), may hold values from -3 to 3
- noise: float32 [32, 64, 3, 128], P('bead', 'space'), may hold values from -6 to 6
- atom_types: int32 [64, 128], P('space'), may hold values from 0 to 3
- occupancy: int32 [64], P('space'), may hold values from 64 to 128, as said below
- type_sigma: float32 [4], replicated, may hold values from 0.2 to 0.4
- type_eps: float32 [4], replicated, may hold values from 0.5 to 2
- type_mass: float32 [4], replicated, may hold values from 1 to 4
Outputs:
- new_positions: float32 [32, 64, 3, 128], P('bead', 'space')
- new_momenta: float32 [32, 64, 3, 128], P('bead', 'space')
Inputs may be any that keep to these rules, and one draw needn't show every extreme that they name: `occupancy`: in each domain of 16 consecutive cells some cell holds 128 atoms.
All inputs are finite; a program needn't handle non-finite values.
Results may differ from a plain program's by a relative error of at most 0.0002.
Values sent between devices are 32-bit elements; how exact they have to be, the bound alone decides.
No kernel may reach another device: no remote copies, remote signals or barrier semaphores. Data moves between devices by JAX's collectives and lax.ppermute only.
A program may use at most 64 MiB of HBM per device.

v0:
```python
import functools

import jax
import jax.numpy as jnp
import numpy as np
from jax import lax
from jax.experimental import pallas as pl
from jax.experimental.pallas import tpu as pltpu
from jax.sharding import PartitionSpec as P

PC = 8
GY = 4
GZ = 4

TIME_STEP = 0.05
INVERSE_TEMP = 32.0
CENTROID_FRICTION = 1.0
INNER_CUT = 0.5
OUTER_CUT = 1.0
CUBE_ROOT_TWO = 2.0 ** (1.0 / 3.0)
F32 = jnp.float32
BF16 = jnp.bfloat16
SPAN = 32
GROUP = 4
STEPS = ((24, 4), (24, 2), (24, 1), (40, 2), (40, 1), (32, 2), (32, 1))
RUN_ROWS = {1: 24, 2: 40}
SPARE = 40
LEAST_LIVE = 64
VMEM_LIMIT = 48 * 1024 * 1024


def mode_matrix(number):
    rows = np.arange(number, dtype=np.float64)[:, None]
    column = np.arange(number, dtype=np.float64)[None, :]
    phases = 2.0 * np.pi * rows * column / number
    factor = np.sqrt(2.0 / number)
    middle = np.cos(np.pi * rows) / np.sqrt(number)
    matrix = np.where(column < number / 2, factor * np.cos(phases), factor * np.sin(phases))
    matrix = np.where(column == number / 2, middle, matrix)
    return np.where(column == 0, 1.0 / np.sqrt(number), matrix)


def contract_matrix(full_count, reduced):
    selected = np.arange(reduced)
    selected = np.where(selected <= reduced // 2, selected, selected + full_count - reduced)
    chosen = mode_matrix(full_count)[:, selected]
    return np.sqrt(reduced / full_count) * (mode_matrix(reduced) @ chosen.T)


def step_matrices(number):
    index = np.arange(number, dtype=np.float64)
    frequency = 2.0 * (number / INVERSE_TEMP) * np.sin(np.pi * index / number)
    friction = np.where(index == 0, CENTROID_FRICTION, 2.0 * frequency)
    damping = np.exp(-friction * TIME_STEP)
    kicking = np.sqrt((1.0 - damping * damping) / INVERSE_TEMP)
    cosine = np.cos(frequency * TIME_STEP)
    sine = np.sin(frequency * TIME_STEP)
    drift = np.where(index == 0, TIME_STEP, sine / np.where(index == 0, 1.0, frequency))
    modes = mode_matrix(number)

    def over_beads(diagonal):
        return (modes * diagonal[None, :]) @ modes.T

    return np.array(
        [
            [over_beads(cosine), over_beads(drift * damping), over_beads(drift * kicking)],
            [
                over_beads(-frequency * sine),
                over_beads(cosine * damping),
                over_beads(cosine * kicking),
            ],
        ]
    )


def partner_lists(domain_cells):
    lists = []
    for one in range(domain_cells):
        near = []
        for two in range(domain_cells):
            step_y, step_z = two // GZ - one // GZ, two % GZ - one % GZ
            if abs(step_y) <= 1 and abs(step_z) <= 1:
                near.append((two, step_y, step_z))
        later = [entry for entry in near if entry[0] > one]
        lists.append(later + [(two + domain_cells, y, z) for two, y, z in near])
    starts = np.cumsum([0] + [len(entries) for entries in lists]).astype(np.int32)
    return starts, np.array([value for entries in lists for entry in entries for value in entry], np.int32)


def long_weight(h, radius_sq, s2):
    inverse = pl.reciprocal(h, approx=True)
    quotient = (CUBE_ROOT_TWO * s2) * inverse
    twice = quotient * quotient * quotient
    outer = jnp.maximum(1.0 - radius_sq, 0.0)
    inner = jnp.maximum(1.0 - 4.0 * radius_sq, 0.0)
    switch = outer * outer - inner * inner
    slope = outer - 4.0 * inner
    return twice * ((twice - 1.0) * (3.0 * (switch * inverse) + slope) - slope)


def short_weight(h, s2):
    inverse = pl.reciprocal(h, approx=True)
    quotient = s2 * inverse
    sixth = quotient * quotient * quotient
    lifted = jnp.maximum((quotient + inverse) - 2.0 / 3.0, 1.0 / 3.0)
    bracket = (sixth - 0.5) * lifted - 1.0 / 6.0
    return (sixth * bracket) * ((lifted - 1.0 / 3.0) * h)


LONG_FACTOR = 4.0
SHORT_SCALE = 1.0 / INNER_CUT
SHORT_FACTOR = 192.0 / SHORT_SCALE


def atom_rows(block, cell):
    return [block[kind, pl.ds(cell, 1), :] for kind in range(3)]


def columns(block):
    few, lanes = block.shape
    return jnp.concatenate([block, jnp.zeros((8 - few, lanes), F32)], axis=0).T


def spread_rows(position, params, cell, rows_ref, size_ref):
    beads, lanes = position.shape[0], position.shape[-1]
    sizes = columns(jnp.concatenate(atom_rows(params, cell)[:2], axis=0))
    for kind in range(2):
        size_ref[cell, kind] = jnp.broadcast_to(sizes[:, kind : kind + 1], (lanes, lanes))
    for bead in range(beads):
        block = columns(jnp.concatenate(atom_rows(position.at[bead], cell), axis=0))
        for axis in range(3):
            rows_ref[cell, bead, axis] = jnp.broadcast_to(
                block[:, axis : axis + 1], (lanes, lanes)
            )


def meet(cell, first, partners, refs):
    lanes_ref, sizes_ref, rows_ref, size_ref, total_ref, back_ref = refs
    beads, lanes = lanes_ref.shape[0], lanes_ref.shape[-1]
    here = pl.ds(first, SPAN)
    tall = (SPAN // 8, 8, lanes)
    row_half = size_ref[cell, 0, here, :].reshape(tall)
    row_root = size_ref[cell, 1, here, :].reshape(tall)
    known = []
    for partner, _, _ in partners:
        half = row_half + sizes_ref[partner, 0]
        s2 = half * half
        known.append((s2, row_root * sizes_ref[partner, 1]))
    for bead in range(beads):
        rows = [rows_ref[cell, bead, axis, here, :].reshape(tall) for axis in range(3)]
        back = [None, None, None]
        for (partner, step_y, step_z), (s2, depth) in zip(partners, known):
            apart = [
                lanes_ref[bead, partner, 0] - rows[0],
                (lanes_ref[bead, partner, 1] + step_y) - rows[1],
                (lanes_ref[bead, partner, 2] + step_z) - rows[2],
            ]
            radius_sq = apart[0] * apart[0] + apart[1] * apart[1] + apart[2] * apart[2]
            weight = depth * long_weight(radius_sq + s2, radius_sq, s2)
            for axis in range(3):
                push = weight * apart[axis]
                back[axis] = push if back[axis] is None else back[axis] + push
                if total_ref is not None:
                    total_ref[partner, bead, axis] += jnp.sum(push, axis=0)
        for axis in range(3):
            value = back[axis].reshape(SPAN, lanes)
            if total_ref is None:
                back_ref[cell, bead, axis, here, :] = value
            else:
                back_ref[cell, bead, axis, here, :] += value


def repeat_lanes(scale, position, params, next_position, next_params, lanes_ref, sizes_ref):
    beads, _, cells, lanes = position.shape

    def per_cell(cell, carry):
        for layer, place, values in ((0, position, params), (1, next_position, next_params)):
            for kind in range(2):
                row = values[kind, pl.ds(cell, 1), :]
                row = scale * row if kind == 0 else row
                sizes_ref[layer * cells + cell, kind] = jnp.broadcast_to(row, (8, lanes))
            for bead in range(beads):
                for axis in range(3):
                    row = place[bead, axis, pl.ds(cell, 1), :]
                    row = scale * (row + 1.0 if layer == 1 and axis == 0 else row)
                    lanes_ref[bead, layer * cells + cell, axis] = jnp.broadcast_to(row, (8, lanes))
        return carry

    lax.fori_loop(0, cells, per_cell, 0)


def fold_back(back_ref, cell, bead):
    lanes = back_ref.shape[-1]
    column = lax.broadcasted_iota(jnp.int32, (lanes, 8), 1)
    sums = [jnp.sum(back_ref[cell, bead, axis], axis=1, keepdims=True) for axis in range(3)]
    block = jnp.where(
        column == 0, sums[0], jnp.where(column == 1, sums[1], jnp.where(column == 2, sums[2], 0.0))
    )
    return block.T[0:3]


def put_rows(out_ref, bead, cell, block):
    for axis in range(3):
        out_ref[bead, axis, pl.ds(cell, 1), :] = block[axis : axis + 1]


def fold_total(total_ref, cell, bead):
    return jnp.concatenate(
        [jnp.sum(total_ref[cell, bead, axis], axis=0, keepdims=True) for axis in range(3)], axis=0
    )


def pairs_kernel(
    plan, occupied, position, params, next_position, next_params,
    force_ref, other_ref, lanes_ref, sizes_ref, rows_ref, size_ref, total_ref, back_ref,
):
    beads, _, cells, lanes = position.shape
    factor = LONG_FACTOR
    together = max(1, 4 // beads)
    repeat_lanes(1.0, position, params, next_position, next_params, lanes_ref, sizes_ref)
    total_ref[...] = jnp.zeros_like(total_ref)

    def spread(index, carry):
        for shift in range(together):
            spread_rows(position, params, index * together + shift, rows_ref, size_ref)
        return carry

    lax.fori_loop(0, cells // together, spread, 0)
    refs = (lanes_ref, sizes_ref, rows_ref, size_ref)

    def entry_of(entry):
        return (
            plan[cells + 1 + 3 * entry],
            plan[cells + 2 + 3 * entry].astype(F32),
            plan[cells + 3 + 3 * entry].astype(F32),
        )

    def per_cell(cell, carry):
        begin, end = plan[cell], plan[cell + 1]
        odd = lax.rem(end - begin, 2)

        most = lanes // SPAN
        needed = lax.div(occupied[cell] + (SPAN - 1), SPAN)
        for parts in (most - 1, most):
            firsts = [part * SPAN for part in range(parts)]

            def all_rows(_, carry, firsts=firsts):
                for first in firsts:
                    meet(cell, first, [(cell, 0.0, 0.0)], refs + (None, back_ref))

                def single(entry, carry):
                    for first in firsts:
                        meet(cell, first, [entry_of(entry)], refs + (total_ref, back_ref))
                    return carry

                def double(step, carry):
                    entry = begin + odd + 2 * step
                    both = [entry_of(entry), entry_of(entry + 1)]
                    for first in firsts:
                        meet(cell, first, both, refs + (total_ref, back_ref))
                    return carry

                carry = lax.fori_loop(begin, begin + odd, single, carry)
                return lax.fori_loop(0, lax.div(end - begin, 2), double, carry)

            full = (needed == most).astype(jnp.int32)
            lax.fori_loop(0, full if parts == most else 1 - full, all_rows, 0)
        return carry

    lax.fori_loop(0, cells, per_cell, 0)

    def finish(index, carry):
        for shift in range(together):
            cell = index * together + shift
            alive = params[1, pl.ds(cell, 1), :] > 0.0
            for bead in range(beads):
                total = fold_total(total_ref, cell, bead) - fold_back(back_ref, cell, bead)
                put_rows(force_ref, bead, cell, jnp.where(alive, factor * total, 0.0))
                put_rows(other_ref, bead, cell, factor * fold_total(total_ref, cell + cells, bead))
        return carry

    lax.fori_loop(0, cells // together, finish, 0)


def octant_key(x, y, z, alive):
    zed = jnp.where(z >= 0.5, 1.0, 0.0)
    gray = jnp.where(y >= 0.5, 3.0 - zed, zed)
    return jnp.where(alive, jnp.where(x >= 0.5, 7.0 - gray, gray), 8.0)


def reach_lists(domain_cells):
    octants = []
    for bit_x in range(2):
        for bit_y in range(2):
            for bit_z in range(2):
                gray = 3 - bit_z if bit_y else bit_z
                octants.append((7 - gray if bit_x else gray, (bit_x, bit_y, bit_z)))
    classes = [[[] for _ in range(domain_cells)] for _ in STEPS]
    for one in range(domain_cells):
        runs = {}
        for layer in range(2):
            for two in range(domain_cells):
                step = (layer, two // GZ - one // GZ, two % GZ - one % GZ)
                if abs(step[1]) > 1 or abs(step[2]) > 1 or (layer == 0 and two <= one):
                    continue
                keys = [
                    key
                    for key, bits in octants
                    if all(move == 0 or bit == (move > 0) for move, bit in zip(step, bits))
                ]
                entry = (two + layer * domain_cells, step[1], step[2], min(keys), max(keys) + 1)
                runs.setdefault(entry[4] - entry[3], []).append(entry)
        for length, entries in sorted(runs.items()):
            entries.sort(key=lambda entry: entry[3:])
            span = RUN_ROWS.get(length, SPAN)
            for place, (rows, count) in enumerate(STEPS):
                if rows == span:
                    whole = len(entries) // count * count
                    classes[place][one] += entries[:whole]
                    entries = entries[whole:]
    starts, values = [], []
    for lists in classes:
        for entries in lists:
            starts.append(len(values) // 5)
            values += [value for entry in entries for value in entry]
        starts.append(len(values) // 5)
    return np.array(starts, np.int32), np.array(values, np.int32)


def split_three(value):
    high = value.astype(BF16).astype(F32)
    rest = value - high
    middle = rest.astype(BF16).astype(F32)
    return high, middle, rest - middle


def order_kernel(position, params, out_ref):
    beads, _, cells, lanes = position.shape
    row = lax.broadcasted_iota(jnp.int32, (lanes, lanes), 0)
    column = lax.broadcasted_iota(jnp.int32, (lanes, lanes), 1)
    before = jnp.where(row < column, 1.0, 0.0).astype(BF16)
    counter = jnp.concatenate([before, jnp.ones((lanes, lanes), BF16)], axis=0)
    kind = lax.broadcasted_iota(jnp.int32, (16, lanes), 0).astype(F32)
    place_row = row.astype(F32)

    def per_cell(index, carry):
        for shift, bead in [(shift, bead) for shift in range(GROUP) for bead in range(beads)]:
            cell = index * GROUP + shift
            sizes = atom_rows(params, cell)[:2]
            place = atom_rows(position.at[bead], cell)
            key = octant_key(*place, sizes[1] > 0.0)
            same = jnp.where(key == kind, 1.0, 0.0)
            less = jnp.where(key < kind, 1.0, 0.0)
            counts = lax.dot_general(
                jnp.concatenate([same, less], axis=1).astype(BF16),
                counter,
                (((1,), (0,)), ((), ())),
                preferred_element_type=F32,
            )
            rank = jnp.sum(same * counts, axis=0, keepdims=True)
            chosen = jnp.where(rank == place_row, 1.0, 0.0).astype(BF16)
            scaled = [SHORT_SCALE * value for value in (*place, sizes[0])]
            block = jnp.concatenate([*scaled, sizes[1], jnp.zeros((3, lanes), F32)], axis=0)
            moved = lax.dot_general(
                jnp.concatenate(split_three(block), axis=0).astype(BF16),
                chosen,
                (((1,), (1,)), ((), ())),
                preferred_element_type=F32,
            )
            out_ref[bead, cell, 0:5, :] = (moved[0:8] + moved[8:16] + moved[16:24])[0:5]
            out_ref[bead, cell, 5:6, :] = rank
            out_ref[bead, cell, 6:8, :] = jnp.zeros((2, lanes), F32)
        return carry

    lax.fori_loop(0, cells // GROUP, per_cell, 0)


def meet_runs(span, local, runs, lanes_ref, sizes_ref, rows_ref, total_ref, back_ref):
    beads, lanes = lanes_ref.shape[0], lanes_ref.shape[-1]
    for bead in range(beads):
        for firsts, partner, step_y, step_z in runs:
            here = pl.ds(firsts[bead], span)
            rows = [
                rows_ref[local, bead, kind, here, :].reshape(span // 8, 8, lanes)
                for kind in range(5)
            ]
            half = rows[3] + sizes_ref[partner, 0]
            s2 = half * half
            apart = [
                lanes_ref[bead, partner, 0] - rows[0],
                (lanes_ref[bead, partner, 1] + step_y) - rows[1],
                (lanes_ref[bead, partner, 2] + step_z) - rows[2],
            ]
            radius_sq = apart[0] * apart[0] + apart[1] * apart[1] + apart[2] * apart[2]
            depth = rows[4] * sizes_ref[partner, 1]
            weight = depth * short_weight(radius_sq + s2, s2)
            for axis in range(3):
                push = weight * apart[axis]
                flat_push = push.reshape(span, lanes)
                if total_ref is None:
                    back_ref[local, bead, axis, here, :] = flat_push
                else:
                    back_ref[local, bead, axis, here, :] += flat_push
                    total_ref[partner, bead, axis] += jnp.sum(push, axis=0)


def reach_kernel(
    plan, position, params, next_position, next_params, ordered, force_ref, other_ref, lanes_ref,
    sizes_ref, rows_ref, total_ref, back_ref,
):
    beads, _, cells, lanes = position.shape
    entries_at = len(STEPS) * (cells + 1)
    bounds_at = plan.shape[0] - beads * cells * 9
    factor = SHORT_FACTOR
    repeat_lanes(SHORT_SCALE, position, params, next_position, next_params, lanes_ref, sizes_ref)
    total_ref[...] = jnp.zeros_like(total_ref)
    rows_ref[:, :, :, lanes:, :] = jnp.zeros((GROUP, beads, 5, SPARE, lanes), F32)
    row = lax.broadcasted_iota(jnp.int32, (lanes, lanes), 0).astype(F32)
    slot = lax.broadcasted_iota(jnp.int32, (8, lanes), 1)
    column = lax.broadcasted_iota(jnp.int32, (lanes, 8), 1)
    refs = (lanes_ref, sizes_ref, rows_ref)
    every = [(local, bead) for local in range(GROUP) for bead in range(beads)]

    def per_group(group, carry):
        for local, bead in every:
            block = ordered[bead, group * GROUP + local].T
            for axis in range(5):
                rows_ref[local, bead, axis, 0:lanes, :] = jnp.broadcast_to(
                    block[:, axis : axis + 1], (lanes, lanes)
                )
            if bead == beads - 1:
                for first in range(0, LEAST_LIVE, SPAN):
                    run = ([first] * beads, group * GROUP + local, 0.0, 0.0)
                    meet_runs(SPAN, local, [run], *refs, None, back_ref)

        def per_cell(local, carry):
            cell = group * GROUP + local

            def bound(bead, octant):
                return plan[bounds_at + (bead * cells + cell) * 9 + octant]

            def itself(index, carry):
                first = pl.multiple_of(index * SPAN, SPAN)
                run = ([first] * beads, cell, 0.0, 0.0)
                meet_runs(SPAN, local, [run], *refs, None, back_ref)
                return carry

            lax.fori_loop(
                LEAST_LIVE // SPAN, lax.div(bound(0, 8) + (SPAN - 1), SPAN), itself, 0
            )

            for place, (span, count) in enumerate(STEPS):
                begin = plan[place * (cells + 1) + cell]
                end = plan[place * (cells + 1) + cell + 1]

                def per_step(step, carry, span=span, count=count, begin=begin):
                    runs, longest = [], 0
                    for shift in range(count):
                        at = entries_at + 5 * (begin + step * count + shift)
                        begins = [
                            lax.bitwise_and(bound(bead, plan[at + 3]), -8) for bead in range(beads)
                        ]
                        for bead in range(beads):
                            longest = jnp.maximum(longest, bound(bead, plan[at + 4]) - begins[bead])
                        runs.append(
                            (
                                begins, plan[at], SHORT_SCALE * plan[at + 1].astype(F32),
                                SHORT_SCALE * plan[at + 2].astype(F32),
                            )
                        )

                    def per_span(index, carry):
                        moved = [
                            (
                                [
                                    pl.multiple_of(jnp.minimum(first + index * span, lanes), 8)
                                    for first in begins
                                ],
                                *rest,
                            )
                            for begins, *rest in runs
                        ]
                        meet_runs(span, local, moved, *refs, total_ref, back_ref)
                        return carry

                    return lax.fori_loop(0, lax.div(longest + (span - 1), span), per_span, carry)

                lax.fori_loop(0, lax.div(end - begin, count), per_step, 0)
            return carry

        lax.fori_loop(0, GROUP, per_cell, 0)

        for local, bead in every:
            cell = group * GROUP + local
            alive = plan[bounds_at + cell * 9 + 8]
            sums = [
                jnp.sum(back_ref[local, bead, axis, 0:lanes, :], axis=1, keepdims=True)
                for axis in range(3)
            ]
            block = jnp.where(
                column == 0,
                sums[0],
                jnp.where(column == 1, sums[1], jnp.where(column == 2, sums[2], 0.0)),
            ).T
            block = jnp.where(slot < alive, block, 0.0)
            chosen = jnp.where(ordered[bead, cell, 5:6, :] == row, 1.0, 0.0).astype(BF16)
            moved = lax.dot_general(
                jnp.concatenate(split_three(block), axis=0).astype(BF16),
                chosen,
                (((1,), (0,)), ((), ())),
                preferred_element_type=F32,
            )
            put_rows(force_ref, bead, cell, (moved[0:8] + moved[8:16] + moved[16:24])[0:3])
        return carry

    lax.fori_loop(0, cells // GROUP, per_group, 0)

    def finish(index, carry):
        for shift, bead in every:
            cell = index * GROUP + shift
            held = jnp.concatenate(atom_rows(force_ref.at[bead], cell), axis=0)
            put_rows(force_ref, bead, cell, factor * (fold_total(total_ref, cell, bead) - held))
            put_rows(other_ref, bead, cell, factor * fold_total(total_ref, cell + cells, bead))
        return carry

    lax.fori_loop(0, cells // GROUP, finish, 0)


def short_forces(position, params, next_position, next_params, ordered, bounds):
    beads, _, cells, lanes = position.shape
    starts, entries = reach_lists(cells)
    plan = jnp.concatenate([jnp.asarray(starts), jnp.asarray(entries), bounds])
    forces = jax.ShapeDtypeStruct((beads, 3, cells, lanes), F32)
    return call(
        reach_kernel,
        (plan, position, params, next_position, next_params, ordered),
        1,
        (forces, forces),
        [
            pltpu.VMEM((beads, 2 * cells, 3, 8, lanes), F32),
            pltpu.VMEM((2 * cells, 2, 8, lanes), F32),
            pltpu.VMEM((GROUP, beads, 5, lanes + SPARE, lanes), F32),
            pltpu.VMEM((2 * cells, beads, 3, 8, lanes), F32),
            pltpu.VMEM((GROUP, beads, 3, lanes + SPARE, lanes), F32),
        ],
        PAIR_FLOPS * beads * 70,
    )


def call(kernel, inputs, smem, outputs, scratch, flops):
    return pl.pallas_call(
        kernel,
        out_shape=outputs,
        in_specs=[
            pl.BlockSpec(memory_space=pltpu.SMEM if place < smem else pltpu.VMEM)
            for place in range(len(inputs))
        ],
        scratch_shapes=scratch,
        compiler_params=pltpu.CompilerParams(vmem_limit_bytes=VMEM_LIMIT),
        cost_estimate=pl.CostEstimate(flops=flops, bytes_accessed=1 << 18, transcendentals=0),
    )(*inputs)


PAIR_FLOPS = 40 * 128 * 128


def pair_forces(position, params, occupied, next_position, next_params):
    beads, _, cells, lanes = position.shape
    starts, entries = partner_lists(cells)
    forces = jax.ShapeDtypeStruct((beads, 3, cells, lanes), F32)
    return call(
        pairs_kernel,
        (
            jnp.asarray(np.concatenate([starts, entries])), occupied, position, params,
            next_position, next_params,
        ),
        2,
        (forces, forces),
        [
            pltpu.VMEM((beads, 2 * cells, 3, 8, lanes), F32),
            pltpu.VMEM((2 * cells, 2, 8, lanes), F32),
            pltpu.VMEM((cells, beads, 3, lanes, lanes), F32),
            pltpu.VMEM((cells, 2, lanes, lanes), F32),
            pltpu.VMEM((2 * cells, beads, 3, 8, lanes), F32),
            pltpu.VMEM((cells, beads, 3, lanes, lanes), F32),
        ],
        PAIR_FLOPS * beads * (len(entries) // 3 + cells),
    )


def kick_kernel(
    piece_rows, groups, table, rank, position, momenta, noise, force, back, params, partial_ref,
    piece_ref, flat_ref,
):
    beads, rows, _ = position.shape
    holders = piece_ref.shape[0]
    reduced = table.shape[0]
    first = rank[0] * beads
    if holders * piece_rows > rows:
        piece_ref[...] = jnp.zeros_like(piece_ref)
    mass = params[2]
    per_root = lax.rsqrt(mass)
    per_root = per_root * (1.5 - 0.5 * mass * per_root * per_root)
    per_mass = jnp.concatenate([1.0 / mass] * 3, axis=0)
    per_root = jnp.concatenate([per_root] * 3, axis=0)
    for bead in range(beads):
        kicked = momenta[bead] + 0.5 * TIME_STEP * (force[bead] + back[bead])
        flat_ref[0, bead] = position[bead]
        flat_ref[1, bead] = kicked * per_mass
        flat_ref[2, bead] = noise[bead] * per_root
    for kind in range(3):
        for bead in range(beads):
            base = (kind * beads + bead) * piece_rows
            for owner in range(holders):
                start = owner * piece_rows
                count = min(piece_rows, rows - start)
                if count > 0:
                    piece_ref[owner, base : base + count, :] = flat_ref[
                        kind, bead, start : start + count, :
                    ]
    for group in range(reduced):
        total = None
        for kind in range(3):
            for bead in range(beads):
                term = table[group, kind * holders * beads + first + bead] * flat_ref[kind, bead]
                total = term if total is None else total + term
        for copy in range(groups):
            partial_ref[group * groups + copy] = total


def move_kernel(piece_rows, beads, matrix, arrived, out_ref, gathered):
    holders = arrived.shape[0]
    taken = 3 * beads
    given = 2 * beads
    for row in range(piece_rows):
        for holder in range(holders):
            gathered[row, holder * taken : (holder + 1) * taken, :] = arrived[
                holder, pl.ds(row, taken, stride=piece_rows), :
            ]
        moved = lax.dot_general(
            matrix[...],
            gathered[row],
            (((1,), (0,)), ((), ())),
            precision=lax.Precision.HIGHEST,
            preferred_element_type=F32,
        )
        for holder in range(holders):
            out_ref[holder, row * given : (row + 1) * given, :] = moved[
                holder * given : (holder + 1) * given
            ]


def finish_kernel(
    piece_rows, groups, table, rank, moved, slow, params, position_ref, momentum_ref, velocity_ref
):
    beads, rows, _ = position_ref.shape
    holders = moved.shape[0]
    given = 2 * beads
    reduced = table.shape[0]
    first = 3 * holders * beads + rank[0] * beads
    mass = jnp.concatenate([params[2]] * 3, axis=0)
    for bead in range(beads):
        for owner in range(holders):
            start = owner * piece_rows
            count = min(piece_rows, rows - start)
            if count > 0:
                position_ref[bead, start : start + count, :] = moved[
                    owner, pl.ds(bead, count, stride=given), :
                ]
                velocity_ref[bead, start : start + count, :] = moved[
                    owner, pl.ds(beads + bead, count, stride=given), :
                ]
    for bead in range(beads):
        total = mass * velocity_ref[bead]
        for group in range(reduced):
            total = total + table[group, first + bead] * slow[group * groups]
        momentum_ref[bead] = total


def shards(positions, momenta, noise, atom_types, occupancy, type_sigma, type_eps, type_mass):
    beads, cells, _, lanes = positions.shape
    holders = lax.axis_size("bead")
    domains = lax.axis_size("space")
    rank = lax.axis_index("bead")
    total_beads = beads * holders
    rows = 3 * cells
    piece_rows = -(-rows // holders)
    held = max(1, PC // holders)
    groups = max(1, holders // PC)
    contract = contract_matrix(total_beads, PC)
    steps = step_matrices(total_beads)
    rank_table = rank.astype(jnp.int32).reshape(1)
    one_back = [((i + 1) % domains, i) for i in range(domains)]
    one_on = [(i, (i + 1) % domains) for i in range(domains)]

    codes = jnp.arange(type_sigma.shape[0])
    onehot = atom_types[..., None] == codes
    living = jnp.arange(lanes)[None, :] < occupancy[:, None]
    half_sigma = 0.5 * jnp.sum(jnp.where(onehot, type_sigma, 0.0), -1)
    root_eps = jnp.sqrt(jnp.sum(jnp.where(onehot, type_eps, 0.0), -1))
    mass = jnp.sum(jnp.where(onehot, type_mass, 0.0), -1)
    params = jnp.stack([half_sigma, jnp.where(living, root_eps, 0.0), mass], 0)
    positions, momenta, noise = (
        value.transpose(0, 2, 1, 3) for value in (positions, momenta, noise)
    )

    stacked = jnp.concatenate([positions, params[None]], 0)
    next_stacked = lax.ppermute(stacked, "space", one_back)
    next_params = next_stacked[beads]
    ordered = call(
        order_kernel,
        (positions, params),
        0,
        jax.ShapeDtypeStruct((beads, cells, 8, lanes), F32),
        [],
        1 << 22,
    )
    key = octant_key(positions[:, 0], positions[:, 1], positions[:, 2], living[None])
    bounds = jnp.sum(
        (key[:, :, None, :] < jnp.arange(9, dtype=F32)[:, None]).astype(jnp.int32), -1
    )
    force, back = short_forces(
        positions, params, next_stacked[:beads], next_params, ordered, bounds.reshape(-1)
    )
    back = lax.ppermute(back, "space", one_on)

    spread = 0.5 * TIME_STEP * (total_beads / PC) * contract
    table = np.concatenate([contract @ steps[0, kind] for kind in range(3)] + [spread], axis=1)
    table = jnp.asarray(table, F32)

    def flat(value):
        return value.reshape(-1, rows, lanes)

    partial, pieces = call(
        functools.partial(kick_kernel, piece_rows, groups),
        (
            table, rank_table, flat(positions), flat(momenta), flat(noise), flat(force), flat(back),
            params,
        ),
        2,
        (
            jax.ShapeDtypeStruct((PC * groups, rows, lanes), F32),
            jax.ShapeDtypeStruct((holders, 3 * beads * piece_rows, lanes), F32),
        ),
        [pltpu.VMEM((3, beads, rows, lanes), F32)],
        1 << 22,
    )
    arrived = lax.all_to_all(
        partial.reshape(holders, held * rows, lanes), "bead", split_axis=0, concat_axis=0, tiled=True
    )
    contracted = jnp.sum(arrived, 0).reshape(held, 3, cells, lanes)
    contracted, pieces = lax.optimization_barrier((contracted, pieces))
    next_contracted = lax.ppermute(contracted, "space", one_back)
    pieces = lax.all_to_all(pieces, "bead", split_axis=0, concat_axis=0, tiled=True)
    slow, slow_back = pair_forces(
        contracted, params, occupancy, next_contracted, next_params
    )
    slow = slow + lax.ppermute(slow_back, "space", one_on)

    order = steps.reshape(2, 3, holders, beads, holders, beads).transpose(2, 0, 3, 4, 1, 5)
    order = order.reshape(2 * total_beads, 3 * total_beads)
    moved = call(
        functools.partial(move_kernel, piece_rows, beads),
        (jnp.asarray(order, F32), pieces),
        0,
        jax.ShapeDtypeStruct((holders, 2 * beads * piece_rows, lanes), F32),
        [pltpu.VMEM((piece_rows, 3 * total_beads, lanes), F32)],
        1 << 23,
    )
    moved_rows = 2 * beads * piece_rows
    sent = jnp.concatenate(
        [
            moved,
            jnp.broadcast_to(slow.reshape(1, held * rows, lanes), (holders, held * rows, lanes)),
        ],
        1,
    )
    got = lax.all_to_all(sent, "bead", split_axis=0, concat_axis=0, tiled=True)
    result = jax.ShapeDtypeStruct((beads, rows, lanes), F32)
    new_positions, new_momenta = call(
        functools.partial(finish_kernel, piece_rows, groups),
        (
            table, rank_table, got[:, :moved_rows],
            got[:, moved_rows:].reshape(holders * held, rows, lanes), params,
        ),
        2,
        (result, result),
        [pltpu.VMEM((beads, rows, lanes), F32)],
        1 << 20,
    )

    def cells_first(value):
        return value.reshape(beads, 3, cells, lanes).transpose(0, 2, 1, 3)

    return cells_first(new_positions), cells_first(new_momenta)


def solution(mesh):
    placed = (
        P("bead", "space", None, None),
        P("bead", "space", None, None),
        P("bead", "space", None, None),
        P("space", None),
        P("space"),
        P(),
        P(),
        P(),
    )
    return jax.shard_map(
        shards,
        mesh=mesh,
        in_specs=placed,
        out_specs=(P("bead", "space", None, None), P("bead", "space", None, None)),
        check_vma=False,
    )
```

profile of v0, /device:TPU:0, one launch (start us, length us, event | category | flops | bytes accessed | tf_op | source)
XLA Modules:
  0.0 128.9 jit_solution(7387868488478948803)
XLA Ops:
  0.6 0.0 copy-start
  0.6 0.8 select_reduce_fusion.2
  1.5 0.7 bitcast_select_fusion
  2.2 0.0 copy-done
  2.2 0.0 copy-start.5
  2.2 2.5 %collective-permute-start = (f32[5,3,16,128]{3,2,1,0:T(8,128)S(1)}, f32[5,3,16,128]{3,2,1,0:T(8,128)S(1)}, u32[]{:S(2)}, u32[]{:S(2)}) collective-permute-start(f32[5,3,16,128]{3,2,1,0:T(8,128)S(1)} %pad_maximum_fusion.1), channel_id=1, source_target_pairs={{1,0},{2,1},{3,2},{0,3},{5,4},{6,5},{7,6},{4,7},{9,8},{10,9},{11,1... | collective-permute-start | bytes 368648 | tf_op jit(solution)/shard_map/ppermute | solution.py:708
  4.7 0.0 copy-done.5
  4.7 0.1 iota_compare_fusion.3
  4.8 0.7 convert_reduce_fusion
  5.5 0.1 copy.24
  5.6 0.0 copy-start.7
  5.6 0.0 copy-start.8
  5.6 0.1 reshape.133
  5.7 0.5 copy-done.7
  6.3 0.0 copy-done.8
  6.3 0.1 concatenate.9.plan
  6.4 6.1 %shard_map.140.ordered = f32[4,16,8,128]{3,2,1,0:T(8,128)S(1)} custom-call(f32[4,3,16,128]{3,2,1,0:T(8,128)S(1)} %bitcast.61, f32[3,16,128]{2,1,0:T(8,128)S(1)} %get-tuple-element.28.params), custom_call_target="tpu_custom_call" | custom-call | flops 4194304 | bytes 262144 | tf_op jit(solution)/shard_map/pallas_call | solution.py:551
  12.5 0.0 collective-permute-done
  12.5 0.0 copy-start.1
  12.5 0.0 copy-start.2
  12.5 42.6 %shard_map.141 = (f32[4,3,16,128]{3,2,1,0:T(8,128)S(1)}, f32[4,3,16,128]{3,2,1,0:T(8,128)S(1)}) custom-call(s32[1405]{0:T(1024)S(1)} %concatenate.9.plan, f32[4,3,16,128]{3,2,1,0:T(8,128)S(1)} %bitcast.62, f32[3,16,128]{2,1,0:T(8,128)S(1)} %get-tuple-element.28.params, f32[4,3,16,128]{3,2,1,0:T(8,128)S(1)} %slice.31.next_position, ...), custom_call_target="tpu_custom_call" | custom-call | flops 183500800 | bytes 262144 | tf_op jit(solution)/shard_map/pallas_call | solution.py:551
  55.1 0.1 collective-permute-start.1
  55.2 4.0 %collective-permute-done.1 = f32[4,3,16,128]{3,2,1,0:T(8,128)S(1)} collective-permute-done((f32[4,3,16,128]{3,2,1,0:T(8,128)S(1)}, f32[4,3,16,128]{3,2,1,0:T(8,128)S(1)}, u32[]{:S(2)}, u32[]{:S(2)}) %collective-permute-start.1) | collective-permute-done | bytes 98336 | tf_op jit(solution)/shard_map/ppermute | solution.py:725
  59.2 0.0 copy-start.4
  59.2 0.0 copy-done.1
  59.2 0.0 copy-done.2
  59.2 0.7 copy-done.4
  59.9 1.5 %shard_map.142 = (f32[8,48,128]{2,1,0:T(8,128)S(1)}, f32[8,72,128]{2,1,0:T(8,128)}) custom-call(f32[8,128]{1,0:T(8,128)S(1)} %copy-done.4, s32[1]{0:T(128)} %bitcast.rank, f32[4,48,128]{2,1,0:T(8,128)S(1)} %bitcast.63, f32[4,48,128]{2,1,0:T(8,128)S(1)} %bitcast.64, f32[4,48,128]{2,1,0:T(8,128)S(1)} %bitcast.65, f32[4,48,128]{2,1,0:T(8,128)S(1)} %bitcast.66, ...), custom_call_target="tpu_custom_call" | custom-call | flops 4194304 | bytes 262144 | tf_op jit(solution)/shard_map/pallas_call | solution.py:551
  61.4 20.4 %all_to_all.15 = f32[8,48,128]{2,1,0:T(8,128)S(1)} all-to-all(f32[8,48,128]{2,1,0:T(8,128)S(1)} %get-tuple-element.14), channel_id=1, replica_groups=mesh['bead'=8,'space'=4] {'bead'}, dimensions={0} | all-to-all | bytes 393216 | tf_op jit(solution)/shard_map/all_to_all | solution.py:748
  81.8 0.0 copy-start.6
  81.8 3.4 %all-to-all-start.1 = ((f32[8,72,128]{2,1,0:T(8,128)}), f32[8,72,128]{2,1,0:T(8,128)S(1)}, u32[]{:S(2)}, u32[]{:S(2)}) async-start(f32[8,72,128]{2,1,0:T(8,128)} %get-tuple-element.16), calls=%async_computation.1 | async-start | bytes 589824 | tf_op jit(solution)/shard_map/all_to_all | solution.py:754
  85.2 0.1 collective-permute-start.2
  85.3 1.5 %collective-permute-done.2.next_position = f32[1,3,16,128]{3,2,1,0:T(8,128)S(1)} collective-permute-done((f32[1,3,16,128]{3,2,1,0:T(8,128)S(1)}, f32[1,3,16,128]{3,2,1,0:T(8,128)S(1)}, u32[]{:S(2)}, u32[]{:S(2)}) %collective-permute-start.2) | collective-permute-done | bytes 24608 | tf_op jit(solution)/shard_map/ppermute | solution.py:753
  86.8 0.0 copy-done.6
  86.8 19.3 %shard_map.144 = (f32[1,3,16,128]{3,2,1,0:T(8,128)S(1)}, f32[1,3,16,128]{3,2,1,0:T(8,128)S(1)}) custom-call(s32[443]{0:T(512)S(1)} %copy-done.6, s32[16]{0:T(128)S(1)} %copy-done.5, f32[1,3,16,128]{3,2,1,0:T(8,128)S(1)} %bitcast.69, f32[3,16,128]{2,1,0:T(8,128)S(1)} %get-tuple-element.28.params, f32[1,3,16,128]{3,2,1,0:T(8,128)S(1)} %collective-permute-done.2.next_position, ...), custom_call_target="tpu_custom_call" | custom-call | flops 103546880 | bytes 262144 | tf_op jit(solution)/shard_map/pallas_call | solution.py:551
  106.1 0.9 collective-permute-start.3
  106.9 2.9 %collective-permute-done.3 = f32[1,3,16,128]{3,2,1,0:T(8,128)S(1)} collective-permute-done((f32[1,3,16,128]{3,2,1,0:T(8,128)S(1)}, f32[1,3,16,128]{3,2,1,0:T(8,128)S(1)}, u32[]{:S(2)}, u32[]{:S(2)}) %collective-permute-start.3) | collective-permute-done | bytes 24608 | tf_op jit(solution)/shard_map/ppermute | solution.py:758
  109.8 0.0 copy-start.3
  109.8 0.0 all-to-all-done.1.arrived
  109.8 0.7 copy-done.3
  110.6 0.4 shard_map.143
  111.0 16.5 %all_to_all.16 = f32[8,96,128]{2,1,0:T(8,128)S(1)} all-to-all(f32[8,96,128]{2,1,0:T(8,128)S(1)} %pad_maximum_fusion), channel_id=1, replica_groups=mesh['bead'=8,'space'=4] {'bead'}, dimensions={0} | all-to-all | bytes 786432 | tf_op jit(solution)/shard_map/all_to_all | solution.py:778
  127.5 1.4 %shard_map.145 = (f32[4,48,128]{2,1,0:T(8,128)}, f32[4,48,128]{2,1,0:T(8,128)}) custom-call(f32[8,128]{1,0:T(8,128)S(1)} %copy-done.4, s32[1]{0:T(128)} %bitcast.rank, f32[8,48,128]{2,1,0:T(8,128)S(1)} %get-tuple-element.26.moved, f32[8,48,128]{2,1,0:T(8,128)S(1)} %get-tuple-element.25.slow, f32[3,16,128]{2,1,0:T(8,128)S(1)} %get-tuple-element.28.params), custom_call_target="tpu_custom_call" | custom-call | flops 1048576 | bytes 262144 | tf_op jit(solution)/shard_map/pallas_call | solution.py:551
  (11 shorter events, 0.2 us)
Async XLA Ops:
  0.6 1.6 %copy-start = (f32[4,16,3,128]{3,1,2,0:T(8,128)S(1)}, f32[4,16,3,128]{3,1,2,0:T(8,128)}, u32[]{:S(2)}) copy-start(f32[4,16,3,128]{3,1,2,0:T(8,128)} %param.13) | copy-start | bytes 294916
  2.2 2.5 %copy-start.5 = (s32[16]{0:T(128)S(1)}, s32[16]{0:T(128)}, u32[]{:S(2)}) copy-start(s32[16]{0:T(128)} %occupied.1) | copy-start | bytes 196
  2.2 10.2 %collective-permute-start = (f32[5,3,16,128]{3,2,1,0:T(8,128)S(1)}, f32[5,3,16,128]{3,2,1,0:T(8,128)S(1)}, u32[]{:S(2)}, u32[]{:S(2)}) collective-permute-start(f32[5,3,16,128]{3,2,1,0:T(8,128)S(1)} %pad_maximum_fusion.1), channel_id=1, source_target_pairs={{1,0},{2,1},{3,2},{0,3},{5,4},{6,5},{7,6},{4,7},{9,8},{10,9},{11,1... | collective-permute-start | bytes 368648 | tf_op jit(solution)/shard_map/ppermute | solution.py:708
  5.6 0.7 copy-start.7
  5.6 0.7 copy-start.8
  12.5 46.7 %copy-start.1 = (f32[4,16,3,128]{3,1,2,0:T(8,128)S(1)}, f32[4,16,3,128]{3,1,2,0:T(8,128)}, u32[]{:S(2)}) copy-start(f32[4,16,3,128]{3,1,2,0:T(8,128)} %param.14) | copy-start | bytes 294916
  12.5 46.7 %copy-start.2 = (f32[4,16,3,128]{3,1,2,0:T(8,128)S(1)}, f32[4,16,3,128]{3,1,2,0:T(8,128)}, u32[]{:S(2)}) copy-start(f32[4,16,3,128]{3,1,2,0:T(8,128)} %param.15) | copy-start | bytes 294916
  55.1 4.1 %collective-permute-start.1 = (f32[4,3,16,128]{3,2,1,0:T(8,128)S(1)}, f32[4,3,16,128]{3,2,1,0:T(8,128)S(1)}, u32[]{:S(2)}, u32[]{:S(2)}) collective-permute-start(f32[4,3,16,128]{3,2,1,0:T(8,128)S(1)} %get-tuple-element.13), channel_id=1, source_target_pairs={{0,1},{1,2},{2,3},{3,0},{4,5},{5,6},{6,7},{7,4},{8,9},{9,10},{10,1... | collective-permute-start | bytes 294920 | tf_op jit(solution)/shard_map/ppermute | solution.py:725
  59.2 0.7 copy-start.4
  81.8 5.0 %copy-start.6 = (s32[443]{0:T(512)S(1)}, s32[443]{0:T(512)}, u32[]{:S(2)}) copy-start(s32[443]{0:T(512)} %constant.34.clone.plan) | copy-start | bytes 5320
  81.8 28.0 %all-to-all-start.1 = ((f32[8,72,128]{2,1,0:T(8,128)}), f32[8,72,128]{2,1,0:T(8,128)S(1)}, u32[]{:S(2)}, u32[]{:S(2)}) async-start(f32[8,72,128]{2,1,0:T(8,128)} %get-tuple-element.16), calls=%async_computation.1 | async-start | bytes 589824 | tf_op jit(solution)/shard_map/all_to_all | solution.py:754
  85.2 1.6 %collective-permute-start.2 = (f32[1,3,16,128]{3,2,1,0:T(8,128)S(1)}, f32[1,3,16,128]{3,2,1,0:T(8,128)S(1)}, u32[]{:S(2)}, u32[]{:S(2)}) collective-permute-start(f32[1,3,16,128]{3,2,1,0:T(8,128)S(1)} %bitcast.68), channel_id=1, source_target_pairs={{1,0},{2,1},{3,2},{0,3},{5,4},{6,5},{7,6},{4,7},{9,8},{10,9},{11,1... | collective-permute-start | bytes 73736 | tf_op jit(solution)/shard_map/ppermute | solution.py:753
  106.1 3.7 %collective-permute-start.3 = (f32[1,3,16,128]{3,2,1,0:T(8,128)S(1)}, f32[1,3,16,128]{3,2,1,0:T(8,128)S(1)}, u32[]{:S(2)}, u32[]{:S(2)}) collective-permute-start(f32[1,3,16,128]{3,2,1,0:T(8,128)S(1)} %get-tuple-element.19), channel_id=1, source_target_pairs={{0,1},{1,2},{2,3},{3,0},{4,5},{5,6},{6,7},{7,4},{8,9},{9,10},{10,1... | collective-permute-start | bytes 73736 | tf_op jit(solution)/shard_map/ppermute | solution.py:758
  109.8 0.8 copy-start.3
where the time goes:
time: 129 us
  Pallas kernels  71.1 us (55%)
  blocking collectives  36.9 us (29%)
  waiting for transfers between devices  8.43 us (7%)
  starting transfers between devices  6.86 us (5%)
  local copies, waits for them, and re-layouts  2.39 us (2%)
  other arithmetic  2.38 us (2%)
    pallas_call x6, Pallas kernels, call(): pl.pallas_call(kernel, out_shape=outputs, in_specs=[pl.BlockSpec(memory_s...  71.1 us
    all_to_all x1, blocking collectives, shards(): lax.all_to_all(partial.reshape(holders, held * rows, lanes), 'bead', spli...  20.4 us
    all_to_all x1, blocking collectives, shards(): got = lax.all_to_all(sent, 'bead', split_axis=0, concat_axis=0, tiled=True)  16.5 us
    ppermute x1, waiting for transfers between devices, shards(): back = lax.ppermute(back, 'space', one_on)  4.02 us
    all_to_all x1, starting transfers between devices, shards(): lax.all_to_all(pieces, 'bead', split_axis=0, concat_axis=0, tiled=True)  3.43 us
    ppermute x1, waiting for transfers between devices, shards(): slow = slow + lax.ppermute(slow_back, 'space', one_on)  2.88 us
  transfers between devices with their start and end apart: 5, of which 3 were waited for; matrix products, arithmetic and copies ran while one was open for 1% of the time, Pallas kernels for 20%

commit v1 on v0

--- a/solution.py
+++ b/solution.py
@@ -25,7 +25,7 @@
 STEPS = ((24, 4), (24, 2), (24, 1), (40, 2), (40, 1), (32, 2), (32, 1))
 RUN_ROWS = {1: 24, 2: 40}
 SPARE = 40
-LEAST_LIVE = 64
+EARLY_ROWS = 96
 VMEM_LIMIT = 48 * 1024 * 1024
 
 
@@ -220,13 +220,17 @@
     repeat_lanes(1.0, position, params, next_position, next_params, lanes_ref, sizes_ref)
     total_ref[...] = jnp.zeros_like(total_ref)
 
+    refs = (lanes_ref, sizes_ref, rows_ref, size_ref)
+
     def spread(index, carry):
         for shift in range(together):
-            spread_rows(position, params, index * together + shift, rows_ref, size_ref)
+            cell = index * together + shift
+            spread_rows(position, params, cell, rows_ref, size_ref)
+            for first in range(0, EARLY_ROWS, SPAN):
+                meet(cell, first, [(cell, 0.0, 0.0)], refs + (None, back_ref))
         return carry
 
     lax.fori_loop(0, cells // together, spread, 0)
-    refs = (lanes_ref, sizes_ref, rows_ref, size_ref)
 
     def entry_of(entry):
         return (
@@ -246,7 +250,8 @@
 
             def all_rows(_, carry, firsts=firsts):
                 for first in firsts:
-                    meet(cell, first, [(cell, 0.0, 0.0)], refs + (None, back_ref))
+                    if first >= EARLY_ROWS:
+                        meet(cell, first, [(cell, 0.0, 0.0)], refs + (None, back_ref))
 
                 def single(entry, carry):
                     for first in firsts:
@@ -429,7 +434,7 @@
                     block[:, axis : axis + 1], (lanes, lanes)
                 )
             if bead == beads - 1:
-                for first in range(0, LEAST_LIVE, SPAN):
+                for first in range(0, EARLY_ROWS, SPAN):
                     run = ([first] * beads, group * GROUP + local, 0.0, 0.0)
                     meet_runs(SPAN, local, [run], *refs, None, back_ref)
 
@@ -446,7 +451,7 @@
                 return carry
 
             lax.fori_loop(
-                LEAST_LIVE // SPAN, lax.div(bound(0, 8) + (SPAN - 1), SPAN), itself, 0
+                EARLY_ROWS // SPAN, lax.div(bound(0, 8) + (SPAN - 1), SPAN), itself, 0
             )
 
             for place, (span, count) in enumerate(STEPS):
@@ -547,14 +552,16 @@
     )
 
 
-def call(kernel, inputs, smem, outputs, scratch, flops):
+def call(kernel, inputs, smem, outputs, scratch, flops, fetched=()):
+    def space(place):
+        if place in fetched:
+            return pltpu.HBM
+        return pltpu.SMEM if place < smem else pltpu.VMEM
+
     return pl.pallas_call(
         kernel,
         out_shape=outputs,
-        in_specs=[
-            pl.BlockSpec(memory_space=pltpu.SMEM if place < smem else pltpu.VMEM)
-            for place in range(len(inputs))
-        ],
+        in_specs=[pl.BlockSpec(memory_space=space(place)) for place in range(len(inputs))],
         scratch_shapes=scratch,
         compiler_params=pltpu.CompilerParams(vmem_limit_bytes=VMEM_LIMIT),
         cost_estimate=pl.CostEstimate(flops=flops, bytes_accessed=1 << 18, transcendentals=0),
@@ -589,9 +596,11 @@
 
 
 def kick_kernel(
-    piece_rows, groups, table, rank, position, momenta, noise, force, back, params, partial_ref,
-    piece_ref, flat_ref,
+    piece_rows, groups, rank, table_hbm, position, momenta, noise, force, back, params, partial_ref,
+    piece_ref, flat_ref, table, done,
 ):
+    fetch = pltpu.make_async_copy(table_hbm, table, done)
+    fetch.start()
     beads, rows, _ = position.shape
     holders = piece_ref.shape[0]
     reduced = table.shape[0]
@@ -618,6 +627,7 @@
                     piece_ref[owner, base : base + count, :] = flat_ref[
                         kind, bead, start : start + count, :
                     ]
+    fetch.wait()
     for group in range(reduced):
         total = None
         for kind in range(3):
@@ -628,7 +638,9 @@
             partial_ref[group * groups + copy] = total
 
 
-def move_kernel(piece_rows, beads, matrix, arrived, out_ref, gathered):
+def move_kernel(piece_rows, beads, matrix_hbm, arrived, out_ref, gathered, matrix, done):
+    fetch = pltpu.make_async_copy(matrix_hbm, matrix, done)
+    fetch.start()
     holders = arrived.shape[0]
     taken = 3 * beads
     given = 2 * beads
@@ -637,6 +649,8 @@
             gathered[row, holder * taken : (holder + 1) * taken, :] = arrived[
                 holder, pl.ds(row, taken, stride=piece_rows), :
             ]
+    fetch.wait()
+    for row in range(piece_rows):
         moved = lax.dot_general(
             matrix[...],
             gathered[row],
@@ -651,8 +665,11 @@
 
 
 def finish_kernel(
-    piece_rows, groups, table, rank, moved, slow, params, position_ref, momentum_ref, velocity_ref
+    piece_rows, groups, rank, table_hbm, moved, slow, params, position_ref, momentum_ref,
+    velocity_ref, table, done,
 ):
+    fetch = pltpu.make_async_copy(table_hbm, table, done)
+    fetch.start()
     beads, rows, _ = position_ref.shape
     holders = moved.shape[0]
     given = 2 * beads
@@ -670,6 +687,7 @@
                 velocity_ref[bead, start : start + count, :] = moved[
                     owner, pl.ds(beads + bead, count, stride=given), :
                 ]
+    fetch.wait()
     for bead in range(beads):
         total = mass * velocity_ref[bead]
         for group in range(reduced):
@@ -734,16 +752,20 @@
     partial, pieces = call(
         functools.partial(kick_kernel, piece_rows, groups),
         (
-            table, rank_table, flat(positions), flat(momenta), flat(noise), flat(force), flat(back),
+            rank_table, table, flat(positions), flat(momenta), flat(noise), flat(force), flat(back),
             params,
         ),
-        2,
+        1,
         (
             jax.ShapeDtypeStruct((PC * groups, rows, lanes), F32),
             jax.ShapeDtypeStruct((holders, 3 * beads * piece_rows, lanes), F32),
         ),
-        [pltpu.VMEM((3, beads, rows, lanes), F32)],
+        [
+            pltpu.VMEM((3, beads, rows, lanes), F32), pltpu.SMEM(table.shape, F32),
+            pltpu.SemaphoreType.DMA,
+        ],
         1 << 22,
+        (1,),
     )
     arrived = lax.all_to_all(
         partial.reshape(holders, held * rows, lanes), "bead", split_axis=0, concat_axis=0, tiled=True
@@ -764,8 +786,12 @@
         (jnp.asarray(order, F32), pieces),
         0,
         jax.ShapeDtypeStruct((holders, 2 * beads * piece_rows, lanes), F32),
-        [pltpu.VMEM((piece_rows, 3 * total_beads, lanes), F32)],
+        [
+            pltpu.VMEM((piece_rows, 3 * total_beads, lanes), F32), pltpu.VMEM(order.shape, F32),
+            pltpu.SemaphoreType.DMA,
+        ],
         1 << 23,
+        (0,),
     )
     moved_rows = 2 * beads * piece_rows
     sent = jnp.concatenate(
@@ -780,13 +806,17 @@
     new_positions, new_momenta = call(
         functools.partial(finish_kernel, piece_rows, groups),
         (
-            table, rank_table, got[:, :moved_rows],
+            rank_table, table, got[:, :moved_rows],
             got[:, moved_rows:].reshape(holders * held, rows, lanes), params,
         ),
-        2,
+        1,
         (result, result),
-        [pltpu.VMEM((beads, rows, lanes), F32)],
+        [
+            pltpu.VMEM((beads, rows, lanes), F32), pltpu.SMEM(table.shape, F32),
+            pltpu.SemaphoreType.DMA,
+        ],
         1 << 20,
+        (1,),
     )
 
     def cells_first(value):

time: 129 us -> 122 us (0.946); the launches traced: 129 us -> 124 us
  blocking collectives: 36.9 us -> 32.3 us
  starting transfers between devices: 6.86 us -> 9.44 us
  waiting for transfers between devices: 8.43 us -> 6.39 us
    all_to_all x1, blocking collectives: 20.4 us -> 13.8 us  [shards(): lax.all_to_all(partial.reshape(holders, held * rows, lanes), 'bead', spli...]
    ppermute x1, starting transfers between devices: 0.85 us -> 3.43 us  [shards(): slow = slow + lax.ppermute(slow_back, 'space', one_on)]
    ppermute x1, waiting for transfers between devices: 2.88 us -> 0.85 us  [shards(): slow = slow + lax.ppermute(slow_back, 'space', one_on)]
    all_to_all x1, blocking collectives: 16.5 us -> 18.4 us  [shards(): got = lax.all_to_all(sent, 'bead', split_axis=0, concat_axis=0, tiled=True)]
where the time goes in v1:
time: 122 us; the launch traced here: 124 us
  Pallas kernels  69.9 us (57%)
  blocking collectives  32.3 us (26%)
  starting transfers between devices  9.44 us (8%)
  waiting for transfers between devices  6.39 us (5%)
  local copies, waits for them, and re-layouts  2.39 us (2%)
  other arithmetic  2.38 us (2%)
    pallas_call x6, Pallas kernels, call(): pl.pallas_call(kernel, out_shape=outputs, in_specs=[pl.BlockSpec(memory_s...  69.9 us
    all_to_all x1, blocking collectives, shards(): got = lax.all_to_all(sent, 'bead', split_axis=0, concat_axis=0, tiled=True)  18.4 us
    all_to_all x1, blocking collectives, shards(): lax.all_to_all(partial.reshape(holders, held * rows, lanes), 'bead', spli...  13.8 us
    ppermute x1, waiting for transfers between devices, shards(): back = lax.ppermute(back, 'space', one_on)  4.02 us
    ppermute x1, starting transfers between devices, shards(): slow = slow + lax.ppermute(slow_back, 'space', one_on)  3.43 us
    all_to_all x1, starting transfers between devices, shards(): lax.all_to_all(pieces, 'bead', split_axis=0, concat_axis=0, tiled=True)  3.43 us
    ppermute x1, starting transfers between devices, shards(): next_stacked = lax.ppermute(stacked, 'space', one_back)  2.46 us
  transfers between devices with their start and end apart: 5, of which 3 were waited for; matrix products, arithmetic and copies ran while one was open for 1% of the time, Pallas kernels for 20%

profile of v1, /device:TPU:0, one launch (start us, length us, event | category | flops | bytes accessed | tf_op | source)
XLA Modules:
  0.0 123.6 jit_solution(9680394839343015318)
XLA Ops:
  0.6 0.0 copy-start
  0.6 0.8 select_reduce_fusion.2
  1.5 0.7 bitcast_select_fusion
  2.2 0.0 copy-done
  2.2 0.0 copy-start.5
  2.2 2.5 %collective-permute-start = (f32[5,3,16,128]{3,2,1,0:T(8,128)S(1)}, f32[5,3,16,128]{3,2,1,0:T(8,128)S(1)}, u32[]{:S(2)}, u32[]{:S(2)}) collective-permute-start(f32[5,3,16,128]{3,2,1,0:T(8,128)S(1)} %pad_maximum_fusion.1), channel_id=1, source_target_pairs={{1,0},{2,1},{3,2},{0,3},{5,4},{6,5},{7,6},{4,7},{9,8},{10,9},{11,1... | collective-permute-start | bytes 368648 | tf_op jit(solution)/shard_map/ppermute | solution.py:726
  4.7 0.0 copy-done.5
  4.7 0.1 iota_compare_fusion.3
  4.8 0.7 convert_reduce_fusion
  5.5 0.1 copy.24
  5.6 0.0 copy-start.7
  5.6 0.0 copy-start.8
  5.6 0.1 reshape.133
  5.7 0.5 copy-done.7
  6.3 0.0 copy-done.8
  6.3 0.1 concatenate.9.plan
  6.4 6.1 %shard_map.140.ordered = f32[4,16,8,128]{3,2,1,0:T(8,128)S(1)} custom-call(f32[4,3,16,128]{3,2,1,0:T(8,128)S(1)} %bitcast.61, f32[3,16,128]{2,1,0:T(8,128)S(1)} %get-tuple-element.28.params), custom_call_target="tpu_custom_call" | custom-call | flops 4194304 | bytes 262144 | tf_op jit(solution)/shard_map/pallas_call | solution.py:561
  12.5 0.0 collective-permute-done
  12.5 0.0 copy-start.1
  12.5 0.0 copy-start.2
  12.5 42.6 %shard_map.141 = (f32[4,3,16,128]{3,2,1,0:T(8,128)S(1)}, f32[4,3,16,128]{3,2,1,0:T(8,128)S(1)}) custom-call(s32[1405]{0:T(1024)S(1)} %concatenate.9.plan, f32[4,3,16,128]{3,2,1,0:T(8,128)S(1)} %bitcast.62, f32[3,16,128]{2,1,0:T(8,128)S(1)} %get-tuple-element.28.params, f32[4,3,16,128]{3,2,1,0:T(8,128)S(1)} %slice.31.next_position, ...), custom_call_target="tpu_custom_call" | custom-call | flops 183500800 | bytes 262144 | tf_op jit(solution)/shard_map/pallas_call | solution.py:561
  55.1 0.1 collective-permute-start.1
  55.2 4.0 %collective-permute-done.1 = f32[4,3,16,128]{3,2,1,0:T(8,128)S(1)} collective-permute-done((f32[4,3,16,128]{3,2,1,0:T(8,128)S(1)}, f32[4,3,16,128]{3,2,1,0:T(8,128)S(1)}, u32[]{:S(2)}, u32[]{:S(2)}) %collective-permute-start.1) | collective-permute-done | bytes 98336 | tf_op jit(solution)/shard_map/ppermute | solution.py:743
  59.2 0.0 copy-start.4
  59.2 0.0 copy-done.1
  59.2 0.0 copy-done.2
  59.2 0.7 copy-done.4
  59.9 1.4 %shard_map.142 = (f32[8,48,128]{2,1,0:T(8,128)S(1)}, f32[8,72,128]{2,1,0:T(8,128)}) custom-call(s32[1]{0:T(128)} %bitcast.rank, f32[8,128]{1,0:T(8,128)S(1)} %copy-done.4, f32[4,48,128]{2,1,0:T(8,128)S(1)} %bitcast.63, f32[4,48,128]{2,1,0:T(8,128)S(1)} %bitcast.64, f32[4,48,128]{2,1,0:T(8,128)S(1)} %bitcast.65, f32[4,48,128]{2,1,0:T(8,128)S(1)} %bitcast.66, ...), custom_call_target="tpu_custom_call" | custom-call | flops 4194304 | bytes 262144 | tf_op jit(solution)/shard_map/pallas_call | solution.py:561
  61.4 13.8 %all_to_all.15 = f32[8,48,128]{2,1,0:T(8,128)S(1)} all-to-all(f32[8,48,128]{2,1,0:T(8,128)S(1)} %get-tuple-element.14), channel_id=1, replica_groups=mesh['bead'=8,'space'=4] {'bead'}, dimensions={0} | all-to-all | bytes 393216 | tf_op jit(solution)/shard_map/all_to_all | solution.py:770
  75.2 0.0 copy-start.6
  75.2 3.4 %all-to-all-start.1 = ((f32[8,72,128]{2,1,0:T(8,128)}), f32[8,72,128]{2,1,0:T(8,128)S(1)}, u32[]{:S(2)}, u32[]{:S(2)}) async-start(f32[8,72,128]{2,1,0:T(8,128)} %get-tuple-element.16), calls=%async_computation.1 | async-start | bytes 589824 | tf_op jit(solution)/shard_map/all_to_all | solution.py:776
  78.7 0.1 collective-permute-start.2
  78.7 1.5 %collective-permute-done.2.next_position = f32[1,3,16,128]{3,2,1,0:T(8,128)S(1)} collective-permute-done((f32[1,3,16,128]{3,2,1,0:T(8,128)S(1)}, f32[1,3,16,128]{3,2,1,0:T(8,128)S(1)}, u32[]{:S(2)}, u32[]{:S(2)}) %collective-permute-start.2) | collective-permute-done | bytes 24608 | tf_op jit(solution)/shard_map/ppermute | solution.py:775
  80.2 0.0 copy-done.6
  80.2 18.1 %shard_map.144 = (f32[1,3,16,128]{3,2,1,0:T(8,128)S(1)}, f32[1,3,16,128]{3,2,1,0:T(8,128)S(1)}) custom-call(s32[443]{0:T(512)S(1)} %copy-done.6, s32[16]{0:T(128)S(1)} %copy-done.5, f32[1,3,16,128]{3,2,1,0:T(8,128)S(1)} %bitcast.69, f32[3,16,128]{2,1,0:T(8,128)S(1)} %get-tuple-element.28.params, f32[1,3,16,128]{3,2,1,0:T(8,128)S(1)} %collective-permute-done.2.next_position, ...), custom_call_target="tpu_custom_call" | custom-call | flops 103546880 | bytes 262144 | tf_op jit(solution)/shard_map/pallas_call | solution.py:561
  98.3 3.4 %collective-permute-start.3 = (f32[1,3,16,128]{3,2,1,0:T(8,128)S(1)}, f32[1,3,16,128]{3,2,1,0:T(8,128)S(1)}, u32[]{:S(2)}, u32[]{:S(2)}) collective-permute-start(f32[1,3,16,128]{3,2,1,0:T(8,128)S(1)} %get-tuple-element.19), channel_id=1, source_target_pairs={{0,1},{1,2},{2,3},{3,0},{4,5},{5,6},{6,7},{7,4},{8,9},{9,10},{10,1... | collective-permute-start | bytes 73736 | tf_op jit(solution)/shard_map/ppermute | solution.py:780
  101.7 0.8 collective-permute-done.3
  102.6 0.0 copy-start.3
  102.6 0.0 all-to-all-done.1.arrived
  102.6 0.7 copy-done.3
  103.3 0.4 shard_map.143
  103.8 18.4 %all_to_all.16 = f32[8,96,128]{2,1,0:T(8,128)S(1)} all-to-all(f32[8,96,128]{2,1,0:T(8,128)S(1)} %pad_maximum_fusion), channel_id=1, replica_groups=mesh['bead'=8,'space'=4] {'bead'}, dimensions={0} | all-to-all | bytes 786432 | tf_op jit(solution)/shard_map/all_to_all | solution.py:804
  122.3 1.3 %shard_map.145 = (f32[4,48,128]{2,1,0:T(8,128)}, f32[4,48,128]{2,1,0:T(8,128)}) custom-call(s32[1]{0:T(128)} %bitcast.rank, f32[8,128]{1,0:T(8,128)S(1)} %copy-done.4, f32[8,48,128]{2,1,0:T(8,128)S(1)} %get-tuple-element.26.moved, f32[8,48,128]{2,1,0:T(8,128)S(1)} %get-tuple-element.25.slow, f32[3,16,128]{2,1,0:T(8,128)S(1)} %get-tuple-element.28.params), custom_call_target="tpu_custom_call" | custom-call | flops 1048576 | bytes 262144 | tf_op jit(solution)/shard_map/pallas_call | solution.py:561
  (11 shorter events, 0.2 us)
Async XLA Ops:
  0.6 1.6 %copy-start = (f32[4,16,3,128]{3,1,2,0:T(8,128)S(1)}, f32[4,16,3,128]{3,1,2,0:T(8,128)}, u32[]{:S(2)}) copy-start(f32[4,16,3,128]{3,1,2,0:T(8,128)} %param.13) | copy-start | bytes 294916
  2.2 2.5 %copy-start.5 = (s32[16]{0:T(128)S(1)}, s32[16]{0:T(128)}, u32[]{:S(2)}) copy-start(s32[16]{0:T(128)} %occupied.1) | copy-start | bytes 196
  2.2 10.2 %collective-permute-start = (f32[5,3,16,128]{3,2,1,0:T(8,128)S(1)}, f32[5,3,16,128]{3,2,1,0:T(8,128)S(1)}, u32[]{:S(2)}, u32[]{:S(2)}) collective-permute-start(f32[5,3,16,128]{3,2,1,0:T(8,128)S(1)} %pad_maximum_fusion.1), channel_id=1, source_target_pairs={{1,0},{2,1},{3,2},{0,3},{5,4},{6,5},{7,6},{4,7},{9,8},{10,9},{11,1... | collective-permute-start | bytes 368648 | tf_op jit(solution)/shard_map/ppermute | solution.py:726
  5.6 0.7 copy-start.7
  5.6 0.7 copy-start.8
  12.5 46.7 %copy-start.1 = (f32[4,16,3,128]{3,1,2,0:T(8,128)S(1)}, f32[4,16,3,128]{3,1,2,0:T(8,128)}, u32[]{:S(2)}) copy-start(f32[4,16,3,128]{3,1,2,0:T(8,128)} %param.14) | copy-start | bytes 294916
  12.5 46.7 %copy-start.2 = (f32[4,16,3,128]{3,1,2,0:T(8,128)S(1)}, f32[4,16,3,128]{3,1,2,0:T(8,128)}, u32[]{:S(2)}) copy-start(f32[4,16,3,128]{3,1,2,0:T(8,128)} %param.15) | copy-start | bytes 294916
  55.1 4.1 %collective-permute-start.1 = (f32[4,3,16,128]{3,2,1,0:T(8,128)S(1)}, f32[4,3,16,128]{3,2,1,0:T(8,128)S(1)}, u32[]{:S(2)}, u32[]{:S(2)}) collective-permute-start(f32[4,3,16,128]{3,2,1,0:T(8,128)S(1)} %get-tuple-element.13), channel_id=1, source_target_pairs={{0,1},{1,2},{2,3},{3,0},{4,5},{5,6},{6,7},{7,4},{8,9},{9,10},{10,1... | collective-permute-start | bytes 294920 | tf_op jit(solution)/shard_map/ppermute | solution.py:743
  59.2 0.7 copy-start.4
  75.2 5.0 %copy-start.6 = (s32[443]{0:T(512)S(1)}, s32[443]{0:T(512)}, u32[]{:S(2)}) copy-start(s32[443]{0:T(512)} %constant.34.clone.plan) | copy-start | bytes 5320
  75.2 27.4 %all-to-all-start.1 = ((f32[8,72,128]{2,1,0:T(8,128)}), f32[8,72,128]{2,1,0:T(8,128)S(1)}, u32[]{:S(2)}, u32[]{:S(2)}) async-start(f32[8,72,128]{2,1,0:T(8,128)} %get-tuple-element.16), calls=%async_computation.1 | async-start | bytes 589824 | tf_op jit(solution)/shard_map/all_to_all | solution.py:776
  78.7 1.6 %collective-permute-start.2 = (f32[1,3,16,128]{3,2,1,0:T(8,128)S(1)}, f32[1,3,16,128]{3,2,1,0:T(8,128)S(1)}, u32[]{:S(2)}, u32[]{:S(2)}) collective-permute-start(f32[1,3,16,128]{3,2,1,0:T(8,128)S(1)} %bitcast.68), channel_id=1, source_target_pairs={{1,0},{2,1},{3,2},{0,3},{5,4},{6,5},{7,6},{4,7},{9,8},{10,9},{11,1... | collective-permute-start | bytes 73736 | tf_op jit(solution)/shard_map/ppermute | solution.py:775
  98.3 4.3 %collective-permute-start.3 = (f32[1,3,16,128]{3,2,1,0:T(8,128)S(1)}, f32[1,3,16,128]{3,2,1,0:T(8,128)S(1)}, u32[]{:S(2)}, u32[]{:S(2)}) collective-permute-start(f32[1,3,16,128]{3,2,1,0:T(8,128)S(1)} %get-tuple-element.19), channel_id=1, source_target_pairs={{0,1},{1,2},{2,3},{3,0},{4,5},{5,6},{6,7},{7,4},{8,9},{9,10},{10,1... | collective-permute-start | bytes 73736 | tf_op jit(solution)/shard_map/ppermute | solution.py:780
  102.6 0.8 copy-start.3

commit v2 on v1

--- a/solution.py
+++ b/solution.py
@@ -339,35 +339,44 @@
     return high, middle, rest - middle
 
 
-def order_kernel(position, params, out_ref):
+def order_kernel(position, params, table, matrix, out_ref, table_out, matrix_out):
     beads, _, cells, lanes = position.shape
+    table_out[...] = table[...]
+    matrix_out[...] = matrix[...]
     row = lax.broadcasted_iota(jnp.int32, (lanes, lanes), 0)
     column = lax.broadcasted_iota(jnp.int32, (lanes, lanes), 1)
     before = jnp.where(row < column, 1.0, 0.0).astype(BF16)
     counter = jnp.concatenate([before, jnp.ones((lanes, lanes), BF16)], axis=0)
     kind = lax.broadcasted_iota(jnp.int32, (16, lanes), 0).astype(F32)
     place_row = row.astype(F32)
-
-    def per_cell(index, carry):
-        for shift, bead in [(shift, bead) for shift in range(GROUP) for bead in range(beads)]:
+    every = [(shift, bead) for shift in range(GROUP) for bead in range(beads)]
+
+    def per_group(index, carry):
+        blocks, sames, marks = [], [], []
+        for shift, bead in every:
             cell = index * GROUP + shift
             sizes = atom_rows(params, cell)[:2]
             place = atom_rows(position.at[bead], cell)
             key = octant_key(*place, sizes[1] > 0.0)
             same = jnp.where(key == kind, 1.0, 0.0)
             less = jnp.where(key < kind, 1.0, 0.0)
-            counts = lax.dot_general(
-                jnp.concatenate([same, less], axis=1).astype(BF16),
-                counter,
-                (((1,), (0,)), ((), ())),
-                preferred_element_type=F32,
+            scaled = [SHORT_SCALE * value for value in (*place, sizes[0])]
+            blocks.append(
+                jnp.concatenate([*scaled, sizes[1], jnp.zeros((3, lanes), F32)], axis=0)
             )
-            rank = jnp.sum(same * counts, axis=0, keepdims=True)
+            sames.append(same)
+            marks.append(jnp.concatenate([same, less], axis=1))
+        counts = jnp.dot(
+            jnp.concatenate(marks, axis=0).astype(BF16), counter, preferred_element_type=F32
+        )
+        for place, (shift, bead) in enumerate(every):
+            cell = index * GROUP + shift
+            rank = jnp.sum(
+                sames[place] * counts[16 * place : 16 * place + 16], axis=0, keepdims=True
+            )
             chosen = jnp.where(rank == place_row, 1.0, 0.0).astype(BF16)
-            scaled = [SHORT_SCALE * value for value in (*place, sizes[0])]
-            block = jnp.concatenate([*scaled, sizes[1], jnp.zeros((3, lanes), F32)], axis=0)
             moved = lax.dot_general(
-                jnp.concatenate(split_three(block), axis=0).astype(BF16),
+                jnp.concatenate(split_three(blocks[place]), axis=0).astype(BF16),
                 chosen,
                 (((1,), (1,)), ((), ())),
                 preferred_element_type=F32,
@@ -377,7 +386,7 @@
             out_ref[bead, cell, 6:8, :] = jnp.zeros((2, lanes), F32)
         return carry
 
-    lax.fori_loop(0, cells // GROUP, per_cell, 0)
+    lax.fori_loop(0, cells // GROUP, per_group, 0)
 
 
 def meet_runs(span, local, runs, lanes_ref, sizes_ref, rows_ref, total_ref, back_ref):
@@ -725,11 +734,19 @@
     stacked = jnp.concatenate([positions, params[None]], 0)
     next_stacked = lax.ppermute(stacked, "space", one_back)
     next_params = next_stacked[beads]
-    ordered = call(
+    spread = 0.5 * TIME_STEP * (total_beads / PC) * contract
+    table = np.concatenate([contract @ steps[0, kind] for kind in range(3)] + [spread], axis=1)
+    order = steps.reshape(2, 3, holders, beads, holders, beads).transpose(2, 0, 3, 4, 1, 5)
+    order = order.reshape(2 * total_beads, 3 * total_beads)
+    ordered, table, order = call(
         order_kernel,
-        (positions, params),
+        (positions, params, jnp.asarray(table, F32), jnp.asarray(order, F32)),
         0,
-        jax.ShapeDtypeStruct((beads, cells, 8, lanes), F32),
+        (
+            jax.ShapeDtypeStruct((beads, cells, 8, lanes), F32),
+            jax.ShapeDtypeStruct(table.shape, F32),
+            jax.ShapeDtypeStruct(order.shape, F32),
+        ),
         [],
         1 << 22,
     )
@@ -741,10 +758,6 @@
         positions, params, next_stacked[:beads], next_params, ordered, bounds.reshape(-1)
     )
     back = lax.ppermute(back, "space", one_on)
-
-    spread = 0.5 * TIME_STEP * (total_beads / PC) * contract
-    table = np.concatenate([contract @ steps[0, kind] for kind in range(3)] + [spread], axis=1)
-    table = jnp.asarray(table, F32)
 
     def flat(value):
         return value.reshape(-1, rows, lanes)
@@ -779,11 +792,9 @@
     )
     slow = slow + lax.ppermute(slow_back, "space", one_on)
 
-    order = steps.reshape(2, 3, holders, beads, holders, beads).transpose(2, 0, 3, 4, 1, 5)
-    order = order.reshape(2 * total_beads, 3 * total_beads)
     moved = call(
         functools.partial(move_kernel, piece_rows, beads),
-        (jnp.asarray(order, F32), pieces),
+        (order, pieces),
         0,
         jax.ShapeDtypeStruct((holders, 2 * beads * piece_rows, lanes), F32),
         [

time: 122 us -> 121 us (level); the launches traced: 124 us -> 121 us
  Pallas kernels: 69.9 us -> 66.5 us
  starting transfers between devices: 9.44 us -> 6.04 us
  blocking collectives: 32.3 us -> 34.9 us
  waiting for transfers between devices: 6.39 us -> 8.78 us
    all_to_all x1, blocking collectives: 13.8 us -> 18.8 us  [shards(): lax.all_to_all(partial.reshape(holders, held * rows, lanes), 'bead', spli...]
    ppermute x1, starting transfers between devices: 3.43 us -> 0.03 us  [shards(): slow = slow + lax.ppermute(slow_back, 'space', one_on)]
    pallas_call x6, Pallas kernels: 69.9 us -> 66.5 us  [call(): pl.pallas_call(kernel, out_shape=outputs, in_specs=[pl.BlockSpec(memory_s...]
    ppermute x1, waiting for transfers between devices: 0.85 us -> 3.24 us  [shards(): slow = slow + lax.ppermute(slow_back, 'space', one_on)]
    all_to_all x1, blocking collectives: 18.4 us -> 16.1 us  [shards(): got = lax.all_to_all(sent, 'bead', split_axis=0, concat_axis=0, tiled=True)]
  transfers between devices with their start and end apart: 5 -> 5, of which waited for: 3 -> 3; matrix products, arithmetic and copies ran while one was open for 1% -> 1% of each run, Pallas kernels for 20% -> 17%
where the time goes in v2:
time: 121 us
  Pallas kernels  66.5 us (55%)
  blocking collectives  34.9 us (29%)
  waiting for transfers between devices  8.78 us (7%)
  starting transfers between devices  6.04 us (5%)
  other arithmetic  2.38 us (2%)
  local copies, waits for them, and re-layouts  1.58 us (1%)
    pallas_call x6, Pallas kernels, call(): pl.pallas_call(kernel, out_shape=outputs, in_specs=[pl.BlockSpec(memory_s...  66.5 us
    all_to_all x1, blocking collectives, shards(): lax.all_to_all(partial.reshape(holders, held * rows, lanes), 'bead', spli...  18.8 us
    all_to_all x1, blocking collectives, shards(): got = lax.all_to_all(sent, 'bead', split_axis=0, concat_axis=0, tiled=True)  16.1 us
    ppermute x1, waiting for transfers between devices, shards(): back = lax.ppermute(back, 'space', one_on)  4.02 us
    all_to_all x1, starting transfers between devices, shards(): lax.all_to_all(pieces, 'bead', split_axis=0, concat_axis=0, tiled=True)  3.43 us
    ppermute x1, waiting for transfers between devices, shards(): slow = slow + lax.ppermute(slow_back, 'space', one_on)  3.24 us
    ppermute x1, starting transfers between devices, shards(): next_stacked = lax.ppermute(stacked, 'space', one_back)  2.46 us
  transfers between devices with their start and end apart: 5, of which 3 were waited for; matrix products, arithmetic and copies ran while one was open for 1% of the time, Pallas kernels for 17%

profile of v2, /device:TPU:0, one launch (start us, length us, event | category | flops | bytes accessed | tf_op | source)
XLA Modules:
  0.0 121.0 jit_solution(15495243117702113732)
XLA Ops:
  0.6 0.0 copy-start
  0.6 0.8 select_reduce_fusion.2
  1.5 0.7 bitcast_select_fusion
  2.2 0.0 copy-done
  2.2 0.0 copy-start.5
  2.2 2.5 %collective-permute-start = (f32[5,3,16,128]{3,2,1,0:T(8,128)S(1)}, f32[5,3,16,128]{3,2,1,0:T(8,128)S(1)}, u32[]{:S(2)}, u32[]{:S(2)}) collective-permute-start(f32[5,3,16,128]{3,2,1,0:T(8,128)S(1)} %pad_maximum_fusion.1), channel_id=1, source_target_pairs={{1,0},{2,1},{3,2},{0,3},{5,4},{6,5},{7,6},{4,7},{9,8},{10,9},{11,1... | collective-permute-start | bytes 368648 | tf_op jit(solution)/shard_map/ppermute | solution.py:735
  4.7 0.0 copy-done.5
  4.7 0.1 iota_compare_fusion.2
  4.8 0.7 convert_reduce_fusion
  5.5 0.0 copy-start.8
  5.5 0.1 copy.24
  5.6 0.0 copy-start.7
  5.6 0.0 copy-start.3
  5.6 0.1 reshape.133
  5.7 0.4 copy-done.8
  6.2 0.1 copy-done.7
  6.3 0.0 copy-start.4
  6.3 0.1 concatenate.9.plan
  6.4 0.0 copy-done.3
  6.4 0.6 copy-done.4
  7.0 2.3 %shard_map.140 = (f32[4,16,8,128]{3,2,1,0:T(8,128)S(1)}, f32[8,128]{1,0:T(8,128)S(1)}, f32[64,96]{1,0:T(8,128)S(1)}) custom-call(f32[4,3,16,128]{3,2,1,0:T(8,128)S(1)} %bitcast.61, f32[3,16,128]{2,1,0:T(8,128)S(1)} %get-tuple-element.34.params, f32[8,128]{1,0:T(8,128)S(1)} %copy-done.4, f32[64,96]{1,0:T(8,128)S(1)} %copy-done.3), custom_call_target="tpu_custom_call" | custom-call | flops 4194304 | bytes 262144 | tf_op jit(solution)/shard_map/pallas_call | solution.py:570
  9.2 0.0 collective-permute-done
  9.3 0.0 copy-start.1
  9.3 0.0 copy-start.2
  9.3 42.2 %shard_map.141 = (f32[4,3,16,128]{3,2,1,0:T(8,128)S(1)}, f32[4,3,16,128]{3,2,1,0:T(8,128)S(1)}) custom-call(s32[1405]{0:T(1024)S(1)} %concatenate.9.plan, f32[4,3,16,128]{3,2,1,0:T(8,128)S(1)} %bitcast.62, f32[3,16,128]{2,1,0:T(8,128)S(1)} %get-tuple-element.34.params, f32[4,3,16,128]{3,2,1,0:T(8,128)S(1)} %slice.31.next_position, ...), custom_call_target="tpu_custom_call" | custom-call | flops 183500800 | bytes 262144 | tf_op jit(solution)/shard_map/pallas_call | solution.py:570
  51.5 0.1 collective-permute-start.1
  51.6 4.0 %collective-permute-done.1 = f32[4,3,16,128]{3,2,1,0:T(8,128)S(1)} collective-permute-done((f32[4,3,16,128]{3,2,1,0:T(8,128)S(1)}, f32[4,3,16,128]{3,2,1,0:T(8,128)S(1)}, u32[]{:S(2)}, u32[]{:S(2)}) %collective-permute-start.1) | collective-permute-done | bytes 98336 | tf_op jit(solution)/shard_map/ppermute | solution.py:760
  55.6 0.0 copy-done.1
  55.6 0.0 copy-done.2
  55.6 1.4 %shard_map.142 = (f32[8,48,128]{2,1,0:T(8,128)S(1)}, f32[8,72,128]{2,1,0:T(8,128)}) custom-call(s32[1]{0:T(128)} %bitcast.rank, f32[8,128]{1,0:T(8,128)S(1)} %get-tuple-element.15.table_hbm, f32[4,48,128]{2,1,0:T(8,128)S(1)} %bitcast.63, f32[4,48,128]{2,1,0:T(8,128)S(1)} %bitcast.64, f32[4,48,128]{2,1,0:T(8,128)S(1)} %bitcast.65, ...), custom_call_target="tpu_custom_call" | custom-call | flops 4194304 | bytes 262144 | tf_op jit(solution)/shard_map/pallas_call | solution.py:570
  57.1 18.8 %all_to_all.15 = f32[8,48,128]{2,1,0:T(8,128)S(1)} all-to-all(f32[8,48,128]{2,1,0:T(8,128)S(1)} %get-tuple-element.20), channel_id=1, replica_groups=mesh['bead'=8,'space'=4] {'bead'}, dimensions={0} | all-to-all | bytes 393216 | tf_op jit(solution)/shard_map/all_to_all | solution.py:783
  75.9 0.0 copy-start.6
  75.9 3.4 %all-to-all-start.1 = ((f32[8,72,128]{2,1,0:T(8,128)}), f32[8,72,128]{2,1,0:T(8,128)S(1)}, u32[]{:S(2)}, u32[]{:S(2)}) async-start(f32[8,72,128]{2,1,0:T(8,128)} %get-tuple-element.22), calls=%async_computation.1 | async-start | bytes 589824 | tf_op jit(solution)/shard_map/all_to_all | solution.py:789
  79.4 0.1 collective-permute-start.2
  79.4 1.5 %collective-permute-done.2.next_position = f32[1,3,16,128]{3,2,1,0:T(8,128)S(1)} collective-permute-done((f32[1,3,16,128]{3,2,1,0:T(8,128)S(1)}, f32[1,3,16,128]{3,2,1,0:T(8,128)S(1)}, u32[]{:S(2)}, u32[]{:S(2)}) %collective-permute-start.2) | collective-permute-done | bytes 24608 | tf_op jit(solution)/shard_map/ppermute | solution.py:788
  81.0 0.0 copy-done.6
  81.0 18.8 %shard_map.144 = (f32[1,3,16,128]{3,2,1,0:T(8,128)S(1)}, f32[1,3,16,128]{3,2,1,0:T(8,128)S(1)}) custom-call(s32[443]{0:T(512)S(1)} %copy-done.6, s32[16]{0:T(128)S(1)} %copy-done.5, f32[1,3,16,128]{3,2,1,0:T(8,128)S(1)} %bitcast.69, f32[3,16,128]{2,1,0:T(8,128)S(1)} %get-tuple-element.34.params, f32[1,3,16,128]{3,2,1,0:T(8,128)S(1)} %collective-permute-done.2.next_position, ...), custom_call_target="tpu_custom_call" | custom-call | flops 103546880 | bytes 262144 | tf_op jit(solution)/shard_map/pallas_call | solution.py:570
  99.8 0.0 collective-permute-start.3
  99.8 3.2 %collective-permute-done.3 = f32[1,3,16,128]{3,2,1,0:T(8,128)S(1)} collective-permute-done((f32[1,3,16,128]{3,2,1,0:T(8,128)S(1)}, f32[1,3,16,128]{3,2,1,0:T(8,128)S(1)}, u32[]{:S(2)}, u32[]{:S(2)}) %collective-permute-start.3) | collective-permute-done | bytes 24608 | tf_op jit(solution)/shard_map/ppermute | solution.py:793
  103.1 0.0 all-to-all-done.1.arrived
  103.1 0.5 shard_map.143
  103.6 16.1 %all_to_all.16 = f32[8,96,128]{2,1,0:T(8,128)S(1)} all-to-all(f32[8,96,128]{2,1,0:T(8,128)S(1)} %pad_maximum_fusion), channel_id=1, replica_groups=mesh['bead'=8,'space'=4] {'bead'}, dimensions={0} | all-to-all | bytes 786432 | tf_op jit(solution)/shard_map/all_to_all | solution.py:815
  119.7 1.3 %shard_map.145 = (f32[4,48,128]{2,1,0:T(8,128)}, f32[4,48,128]{2,1,0:T(8,128)}) custom-call(s32[1]{0:T(128)} %bitcast.rank, f32[8,128]{1,0:T(8,128)S(1)} %get-tuple-element.15.table_hbm, f32[8,48,128]{2,1,0:T(8,128)S(1)} %get-tuple-element.32.moved, f32[8,48,128]{2,1,0:T(8,128)S(1)} %get-tuple-element.31.slow, f32[3,16,128]{2,1,0:T(8,128)S(1)} %get-tuple-element.34.params), custom_call_target="tpu_custom_call" | custom-call | flops 1048576 | bytes 262144 | tf_op jit(solution)/shard_map/pallas_call | solution.py:570
  (11 shorter events, 0.2 us)
Async XLA Ops:
  0.6 1.6 %copy-start = (f32[4,16,3,128]{3,1,2,0:T(8,128)S(1)}, f32[4,16,3,128]{3,1,2,0:T(8,128)}, u32[]{:S(2)}) copy-start(f32[4,16,3,128]{3,1,2,0:T(8,128)} %param.13) | copy-start | bytes 294916
  2.2 2.5 %copy-start.5 = (s32[16]{0:T(128)S(1)}, s32[16]{0:T(128)}, u32[]{:S(2)}) copy-start(s32[16]{0:T(128)} %occupied.1) | copy-start | bytes 196
  2.2 7.0 %collective-permute-start = (f32[5,3,16,128]{3,2,1,0:T(8,128)S(1)}, f32[5,3,16,128]{3,2,1,0:T(8,128)S(1)}, u32[]{:S(2)}, u32[]{:S(2)}) collective-permute-start(f32[5,3,16,128]{3,2,1,0:T(8,128)S(1)} %pad_maximum_fusion.1), channel_id=1, source_target_pairs={{1,0},{2,1},{3,2},{0,3},{5,4},{6,5},{7,6},{4,7},{9,8},{10,9},{11,1... | collective-permute-start | bytes 368648 | tf_op jit(solution)/shard_map/ppermute | solution.py:735
  5.5 0.7 copy-start.8
  5.6 0.7 copy-start.7
  5.6 0.8 copy-start.3
  6.3 0.7 copy-start.4
  9.3 46.3 %copy-start.1 = (f32[4,16,3,128]{3,1,2,0:T(8,128)S(1)}, f32[4,16,3,128]{3,1,2,0:T(8,128)}, u32[]{:S(2)}) copy-start(f32[4,16,3,128]{3,1,2,0:T(8,128)} %param.14) | copy-start | bytes 294916
  9.3 46.3 %copy-start.2 = (f32[4,16,3,128]{3,1,2,0:T(8,128)S(1)}, f32[4,16,3,128]{3,1,2,0:T(8,128)}, u32[]{:S(2)}) copy-start(f32[4,16,3,128]{3,1,2,0:T(8,128)} %param.15) | copy-start | bytes 294916
  51.5 4.1 %collective-permute-start.1 = (f32[4,3,16,128]{3,2,1,0:T(8,128)S(1)}, f32[4,3,16,128]{3,2,1,0:T(8,128)S(1)}, u32[]{:S(2)}, u32[]{:S(2)}) collective-permute-start(f32[4,3,16,128]{3,2,1,0:T(8,128)S(1)} %get-tuple-element.19), channel_id=1, source_target_pairs={{0,1},{1,2},{2,3},{3,0},{4,5},{5,6},{6,7},{7,4},{8,9},{9,10},{10,1... | collective-permute-start | bytes 294920 | tf_op jit(solution)/shard_map/ppermute | solution.py:760
  75.9 5.0 %copy-start.6 = (s32[443]{0:T(512)S(1)}, s32[443]{0:T(512)}, u32[]{:S(2)}) copy-start(s32[443]{0:T(512)} %constant.35.clone.plan) | copy-start | bytes 5320
  75.9 27.1 %all-to-all-start.1 = ((f32[8,72,128]{2,1,0:T(8,128)}), f32[8,72,128]{2,1,0:T(8,128)S(1)}, u32[]{:S(2)}, u32[]{:S(2)}) async-start(f32[8,72,128]{2,1,0:T(8,128)} %get-tuple-element.22), calls=%async_computation.1 | async-start | bytes 589824 | tf_op jit(solution)/shard_map/all_to_all | solution.py:789
  79.4 1.6 %collective-permute-start.2 = (f32[1,3,16,128]{3,2,1,0:T(8,128)S(1)}, f32[1,3,16,128]{3,2,1,0:T(8,128)S(1)}, u32[]{:S(2)}, u32[]{:S(2)}) collective-permute-start(f32[1,3,16,128]{3,2,1,0:T(8,128)S(1)} %bitcast.68), channel_id=1, source_target_pairs={{1,0},{2,1},{3,2},{0,3},{5,4},{6,5},{7,6},{4,7},{9,8},{10,9},{11,1... | collective-permute-start | bytes 73736 | tf_op jit(solution)/shard_map/ppermute | solution.py:788
  99.8 3.3 %collective-permute-start.3 = (f32[1,3,16,128]{3,2,1,0:T(8,128)S(1)}, f32[1,3,16,128]{3,2,1,0:T(8,128)S(1)}, u32[]{:S(2)}, u32[]{:S(2)}) collective-permute-start(f32[1,3,16,128]{3,2,1,0:T(8,128)S(1)} %get-tuple-element.25), channel_id=1, source_target_pairs={{0,1},{1,2},{2,3},{3,0},{4,5},{5,6},{6,7},{7,4},{8,9},{9,10},{10,1... | collective-permute-start | bytes 73736 | tf_op jit(solution)/shard_map/ppermute | solution.py:793

commit v3 on v2

--- a/solution.py
+++ b/solution.py
@@ -22,10 +22,9 @@
 BF16 = jnp.bfloat16
 SPAN = 32
 GROUP = 4
-STEPS = ((24, 4), (24, 2), (24, 1), (40, 2), (40, 1), (32, 2), (32, 1))
-RUN_ROWS = {1: 24, 2: 40}
-SPARE = 40
-EARLY_ROWS = 96
+STEPS = ((24, 4), (24, 2), (24, 1), (40, 2), (40, 1), (32, 2), (32, 1), (96, 1))
+RUN_ROWS = {1: 24, 2: 40, 6: 96}
+SPARE = 96
 VMEM_LIMIT = 48 * 1024 * 1024
 
 
@@ -226,7 +225,7 @@
         for shift in range(together):
             cell = index * together + shift
             spread_rows(position, params, cell, rows_ref, size_ref)
-            for first in range(0, EARLY_ROWS, SPAN):
+            for first in range(0, lanes, SPAN):
                 meet(cell, first, [(cell, 0.0, 0.0)], refs + (None, back_ref))
         return carry
 
@@ -249,10 +248,6 @@
             firsts = [part * SPAN for part in range(parts)]
 
             def all_rows(_, carry, firsts=firsts):
-                for first in firsts:
-                    if first >= EARLY_ROWS:
-                        meet(cell, first, [(cell, 0.0, 0.0)], refs + (None, back_ref))
-
                 def single(entry, carry):
                     for first in firsts:
                         meet(cell, first, [entry_of(entry)], refs + (total_ref, back_ref))
@@ -391,9 +386,17 @@
 
 def meet_runs(span, local, runs, lanes_ref, sizes_ref, rows_ref, total_ref, back_ref):
     beads, lanes = lanes_ref.shape[0], lanes_ref.shape[-1]
+    if span > 2 * SPAN:
+        for start in range(0, span, SPAN):
+            later = [([first + start for first in firsts], *rest) for firsts, *rest in runs]
+            meet_runs(
+                SPAN, local, later, lanes_ref, sizes_ref, rows_ref, total_ref, back_ref
+            )
+        return
     for bead in range(beads):
         for firsts, partner, step_y, step_z in runs:
-            here = pl.ds(firsts[bead], span)
+            first = firsts[bead]
+            here = pl.ds(first if isinstance(first, int) else pl.multiple_of(first, 8), span)
             rows = [
                 rows_ref[local, bead, kind, here, :].reshape(span // 8, 8, lanes)
                 for kind in range(5)
@@ -443,7 +446,7 @@
                     block[:, axis : axis + 1], (lanes, lanes)
                 )
             if bead == beads - 1:
-                for first in range(0, EARLY_ROWS, SPAN):
+                for first in range(0, lanes, SPAN):
                     run = ([first] * beads, group * GROUP + local, 0.0, 0.0)
                     meet_runs(SPAN, local, [run], *refs, None, back_ref)
 
@@ -452,16 +455,6 @@
 
             def bound(bead, octant):
                 return plan[bounds_at + (bead * cells + cell) * 9 + octant]
-
-            def itself(index, carry):
-                first = pl.multiple_of(index * SPAN, SPAN)
-                run = ([first] * beads, cell, 0.0, 0.0)
-                meet_runs(SPAN, local, [run], *refs, None, back_ref)
-                return carry
-
-            lax.fori_loop(
-                EARLY_ROWS // SPAN, lax.div(bound(0, 8) + (SPAN - 1), SPAN), itself, 0
-            )
 
             for place, (span, count) in enumerate(STEPS):
                 begin = plan[place * (cells + 1) + cell]

time: 121 us -> 119 us (0.983); the launches traced: 121 us -> 117 us
  blocking collectives: 34.9 us -> 31.5 us
  Pallas kernels: 66.5 us -> 64.6 us
  waiting for transfers between devices: 8.78 us -> 9.99 us
    all_to_all x1, blocking collectives: 18.8 us -> 15.1 us  [shards(): lax.all_to_all(partial.reshape(holders, held * rows, lanes), 'bead', spli...]
    pallas_call x6, Pallas kernels: 66.5 us -> 64.6 us  [call(): pl.pallas_call(kernel, out_shape=outputs, in_specs=[pl.BlockSpec(memory_s...]
    ppermute x1, waiting for transfers between devices: 4.02 us -> 5.45 us  [shards(): back = lax.ppermute(back, 'space', one_on)]
  transfers between devices with their start and end apart: 5 -> 5, of which waited for: 3 -> 3; matrix products, arithmetic and copies ran while one was open for 1% -> 1% of each run, Pallas kernels for 17% -> 18%
where the time goes in v3:
time: 119 us; the launch traced here: 117 us
  Pallas kernels  64.6 us (54%)
  blocking collectives  31.5 us (26%)
  waiting for transfers between devices  9.99 us (8%)
  starting transfers between devices  6.26 us (5%)
  other arithmetic  2.38 us (2%)
  local copies, waits for them, and re-layouts  1.58 us (1%)
    pallas_call x6, Pallas kernels, call(): pl.pallas_call(kernel, out_shape=outputs, in_specs=[pl.BlockSpec(memory_s...  64.6 us
    all_to_all x1, blocking collectives, shards(): got = lax.all_to_all(sent, 'bead', split_axis=0, concat_axis=0, tiled=True)  16.4 us
    all_to_all x1, blocking collectives, shards(): lax.all_to_all(partial.reshape(holders, held * rows, lanes), 'bead', spli...  15.1 us
    ppermute x1, waiting for transfers between devices, shards(): back = lax.ppermute(back, 'space', one_on)  5.45 us
    all_to_all x1, starting transfers between devices, shards(): lax.all_to_all(pieces, 'bead', split_axis=0, concat_axis=0, tiled=True)  3.43 us
    ppermute x1, waiting for transfers between devices, shards(): slow = slow + lax.ppermute(slow_back, 'space', one_on)  3.02 us
    ppermute x1, starting transfers between devices, shards(): next_stacked = lax.ppermute(stacked, 'space', one_back)  2.46 us
  transfers between devices with their start and end apart: 5, of which 3 were waited for; matrix products, arithmetic and copies ran while one was open for 1% of the time, Pallas kernels for 18%

profile of v3, /device:TPU:0, one launch (start us, length us, event | category | flops | bytes accessed | tf_op | source)
XLA Modules:
  0.0 117.2 jit_solution(15517556464202944212)
XLA Ops:
  0.6 0.0 copy-start
  0.6 0.8 select_reduce_fusion.2
  1.5 0.7 bitcast_select_fusion
  2.2 0.0 copy-done
  2.2 0.0 copy-start.5
  2.2 2.5 %collective-permute-start = (f32[5,3,16,128]{3,2,1,0:T(8,128)S(1)}, f32[5,3,16,128]{3,2,1,0:T(8,128)S(1)}, u32[]{:S(2)}, u32[]{:S(2)}) collective-permute-start(f32[5,3,16,128]{3,2,1,0:T(8,128)S(1)} %pad_maximum_fusion.1), channel_id=1, source_target_pairs={{1,0},{2,1},{3,2},{0,3},{5,4},{6,5},{7,6},{4,7},{9,8},{10,9},{11,1... | collective-permute-start | bytes 368648 | tf_op jit(solution)/shard_map/ppermute | solution.py:728
  4.7 0.0 copy-done.5
  4.7 0.1 iota_compare_fusion.2
  4.8 0.7 convert_reduce_fusion
  5.5 0.0 copy-start.8
  5.5 0.1 copy.24
  5.6 0.0 copy-start.7
  5.6 0.0 copy-start.3
  5.6 0.1 reshape.133
  5.7 0.4 copy-done.8
  6.2 0.1 copy-done.7
  6.3 0.0 copy-start.4
  6.3 0.1 concatenate.9.plan
  6.4 0.0 copy-done.3
  6.4 0.6 copy-done.4
  7.0 2.3 %shard_map.140 = (f32[4,16,8,128]{3,2,1,0:T(8,128)S(1)}, f32[8,128]{1,0:T(8,128)S(1)}, f32[64,96]{1,0:T(8,128)S(1)}) custom-call(f32[4,3,16,128]{3,2,1,0:T(8,128)S(1)} %bitcast.61, f32[3,16,128]{2,1,0:T(8,128)S(1)} %get-tuple-element.34.params, f32[8,128]{1,0:T(8,128)S(1)} %copy-done.4, f32[64,96]{1,0:T(8,128)S(1)} %copy-done.3), custom_call_target="tpu_custom_call" | custom-call | flops 4194304 | bytes 262144 | tf_op jit(solution)/shard_map/pallas_call | solution.py:563
  9.2 0.0 collective-permute-done
  9.3 0.0 copy-start.1
  9.3 0.0 copy-start.2
  9.3 40.6 %shard_map.141 = (f32[4,3,16,128]{3,2,1,0:T(8,128)S(1)}, f32[4,3,16,128]{3,2,1,0:T(8,128)S(1)}) custom-call(s32[1422]{0:T(1024)S(1)} %concatenate.9.plan, f32[4,3,16,128]{3,2,1,0:T(8,128)S(1)} %bitcast.62, f32[3,16,128]{2,1,0:T(8,128)S(1)} %get-tuple-element.34.params, f32[4,3,16,128]{3,2,1,0:T(8,128)S(1)} %slice.31.next_position, ...), custom_call_target="tpu_custom_call" | custom-call | flops 183500800 | bytes 262144 | tf_op jit(solution)/shard_map/pallas_call | solution.py:563
  49.9 0.1 collective-permute-start.1
  50.0 5.4 %collective-permute-done.1 = f32[4,3,16,128]{3,2,1,0:T(8,128)S(1)} collective-permute-done((f32[4,3,16,128]{3,2,1,0:T(8,128)S(1)}, f32[4,3,16,128]{3,2,1,0:T(8,128)S(1)}, u32[]{:S(2)}, u32[]{:S(2)}) %collective-permute-start.1) | collective-permute-done | bytes 98336 | tf_op jit(solution)/shard_map/ppermute | solution.py:753
  55.4 0.0 copy-done.1
  55.4 0.0 copy-done.2
  55.4 1.4 %shard_map.142 = (f32[8,48,128]{2,1,0:T(8,128)S(1)}, f32[8,72,128]{2,1,0:T(8,128)}) custom-call(s32[1]{0:T(128)} %bitcast.rank, f32[8,128]{1,0:T(8,128)S(1)} %get-tuple-element.15.table_hbm, f32[4,48,128]{2,1,0:T(8,128)S(1)} %bitcast.63, f32[4,48,128]{2,1,0:T(8,128)S(1)} %bitcast.64, f32[4,48,128]{2,1,0:T(8,128)S(1)} %bitcast.65, ...), custom_call_target="tpu_custom_call" | custom-call | flops 4194304 | bytes 262144 | tf_op jit(solution)/shard_map/pallas_call | solution.py:563
  56.9 15.1 %all_to_all.15 = f32[8,48,128]{2,1,0:T(8,128)S(1)} all-to-all(f32[8,48,128]{2,1,0:T(8,128)S(1)} %get-tuple-element.20), channel_id=1, replica_groups=mesh['bead'=8,'space'=4] {'bead'}, dimensions={0} | all-to-all | bytes 393216 | tf_op jit(solution)/shard_map/all_to_all | solution.py:776
  72.0 0.0 copy-start.6
  72.1 3.4 %all-to-all-start.1 = ((f32[8,72,128]{2,1,0:T(8,128)}), f32[8,72,128]{2,1,0:T(8,128)S(1)}, u32[]{:S(2)}, u32[]{:S(2)}) async-start(f32[8,72,128]{2,1,0:T(8,128)} %get-tuple-element.22), calls=%async_computation.1 | async-start | bytes 589824 | tf_op jit(solution)/shard_map/all_to_all | solution.py:782
  75.5 0.1 collective-permute-start.2
  75.6 1.5 %collective-permute-done.2.next_position = f32[1,3,16,128]{3,2,1,0:T(8,128)S(1)} collective-permute-done((f32[1,3,16,128]{3,2,1,0:T(8,128)S(1)}, f32[1,3,16,128]{3,2,1,0:T(8,128)S(1)}, u32[]{:S(2)}, u32[]{:S(2)}) %collective-permute-start.2) | collective-permute-done | bytes 24608 | tf_op jit(solution)/shard_map/ppermute | solution.py:781
  77.1 0.0 copy-done.6
  77.1 18.6 %shard_map.144 = (f32[1,3,16,128]{3,2,1,0:T(8,128)S(1)}, f32[1,3,16,128]{3,2,1,0:T(8,128)S(1)}) custom-call(s32[443]{0:T(512)S(1)} %copy-done.6, s32[16]{0:T(128)S(1)} %copy-done.5, f32[1,3,16,128]{3,2,1,0:T(8,128)S(1)} %bitcast.69, f32[3,16,128]{2,1,0:T(8,128)S(1)} %get-tuple-element.34.params, f32[1,3,16,128]{3,2,1,0:T(8,128)S(1)} %collective-permute-done.2.next_position, ...), custom_call_target="tpu_custom_call" | custom-call | flops 103546880 | bytes 262144 | tf_op jit(solution)/shard_map/pallas_call | solution.py:563
  95.7 0.3 collective-permute-start.3
  95.9 3.0 %collective-permute-done.3 = f32[1,3,16,128]{3,2,1,0:T(8,128)S(1)} collective-permute-done((f32[1,3,16,128]{3,2,1,0:T(8,128)S(1)}, f32[1,3,16,128]{3,2,1,0:T(8,128)S(1)}, u32[]{:S(2)}, u32[]{:S(2)}) %collective-permute-start.3) | collective-permute-done | bytes 24608 | tf_op jit(solution)/shard_map/ppermute | solution.py:786
  98.9 0.0 all-to-all-done.1.arrived
  98.9 0.5 shard_map.143
  99.5 16.4 %all_to_all.16 = f32[8,96,128]{2,1,0:T(8,128)S(1)} all-to-all(f32[8,96,128]{2,1,0:T(8,128)S(1)} %pad_maximum_fusion), channel_id=1, replica_groups=mesh['bead'=8,'space'=4] {'bead'}, dimensions={0} | all-to-all | bytes 786432 | tf_op jit(solution)/shard_map/all_to_all | solution.py:808
  115.8 1.3 %shard_map.145 = (f32[4,48,128]{2,1,0:T(8,128)}, f32[4,48,128]{2,1,0:T(8,128)}) custom-call(s32[1]{0:T(128)} %bitcast.rank, f32[8,128]{1,0:T(8,128)S(1)} %get-tuple-element.15.table_hbm, f32[8,48,128]{2,1,0:T(8,128)S(1)} %get-tuple-element.32.moved, f32[8,48,128]{2,1,0:T(8,128)S(1)} %get-tuple-element.31.slow, f32[3,16,128]{2,1,0:T(8,128)S(1)} %get-tuple-element.34.params), custom_call_target="tpu_custom_call" | custom-call | flops 1048576 | bytes 262144 | tf_op jit(solution)/shard_map/pallas_call | solution.py:563
  (11 shorter events, 0.2 us)
Async XLA Ops:
  0.6 1.6 %copy-start = (f32[4,16,3,128]{3,1,2,0:T(8,128)S(1)}, f32[4,16,3,128]{3,1,2,0:T(8,128)}, u32[]{:S(2)}) copy-start(f32[4,16,3,128]{3,1,2,0:T(8,128)} %param.13) | copy-start | bytes 294916
  2.2 2.5 %copy-start.5 = (s32[16]{0:T(128)S(1)}, s32[16]{0:T(128)}, u32[]{:S(2)}) copy-start(s32[16]{0:T(128)} %occupied.1) | copy-start | bytes 196
  2.2 7.0 %collective-permute-start = (f32[5,3,16,128]{3,2,1,0:T(8,128)S(1)}, f32[5,3,16,128]{3,2,1,0:T(8,128)S(1)}, u32[]{:S(2)}, u32[]{:S(2)}) collective-permute-start(f32[5,3,16,128]{3,2,1,0:T(8,128)S(1)} %pad_maximum_fusion.1), channel_id=1, source_target_pairs={{1,0},{2,1},{3,2},{0,3},{5,4},{6,5},{7,6},{4,7},{9,8},{10,9},{11,1... | collective-permute-start | bytes 368648 | tf_op jit(solution)/shard_map/ppermute | solution.py:728
  5.5 0.7 copy-start.8
  5.6 0.7 copy-start.7
  5.6 0.8 copy-start.3
  6.3 0.7 copy-start.4
  9.3 46.1 %copy-start.1 = (f32[4,16,3,128]{3,1,2,0:T(8,128)S(1)}, f32[4,16,3,128]{3,1,2,0:T(8,128)}, u32[]{:S(2)}) copy-start(f32[4,16,3,128]{3,1,2,0:T(8,128)} %param.14) | copy-start | bytes 294916
  9.3 46.1 %copy-start.2 = (f32[4,16,3,128]{3,1,2,0:T(8,128)S(1)}, f32[4,16,3,128]{3,1,2,0:T(8,128)}, u32[]{:S(2)}) copy-start(f32[4,16,3,128]{3,1,2,0:T(8,128)} %param.15) | copy-start | bytes 294916
  49.9 5.5 %collective-permute-start.1 = (f32[4,3,16,128]{3,2,1,0:T(8,128)S(1)}, f32[4,3,16,128]{3,2,1,0:T(8,128)S(1)}, u32[]{:S(2)}, u32[]{:S(2)}) collective-permute-start(f32[4,3,16,128]{3,2,1,0:T(8,128)S(1)} %get-tuple-element.19), channel_id=1, source_target_pairs={{0,1},{1,2},{2,3},{3,0},{4,5},{5,6},{6,7},{7,4},{8,9},{9,10},{10,1... | collective-permute-start | bytes 294920 | tf_op jit(solution)/shard_map/ppermute | solution.py:753
  72.0 5.0 %copy-start.6 = (s32[443]{0:T(512)S(1)}, s32[443]{0:T(512)}, u32[]{:S(2)}) copy-start(s32[443]{0:T(512)} %constant.35.clone.plan) | copy-start | bytes 5320
  72.1 26.9 %all-to-all-start.1 = ((f32[8,72,128]{2,1,0:T(8,128)}), f32[8,72,128]{2,1,0:T(8,128)S(1)}, u32[]{:S(2)}, u32[]{:S(2)}) async-start(f32[8,72,128]{2,1,0:T(8,128)} %get-tuple-element.22), calls=%async_computation.1 | async-start | bytes 589824 | tf_op jit(solution)/shard_map/all_to_all | solution.py:782
  75.5 1.6 %collective-permute-start.2 = (f32[1,3,16,128]{3,2,1,0:T(8,128)S(1)}, f32[1,3,16,128]{3,2,1,0:T(8,128)S(1)}, u32[]{:S(2)}, u32[]{:S(2)}) collective-permute-start(f32[1,3,16,128]{3,2,1,0:T(8,128)S(1)} %bitcast.68), channel_id=1, source_target_pairs={{1,0},{2,1},{3,2},{0,3},{5,4},{6,5},{7,6},{4,7},{9,8},{10,9},{11,1... | collective-permute-start | bytes 73736 | tf_op jit(solution)/shard_map/ppermute | solution.py:781
  95.7 3.3 %collective-permute-start.3 = (f32[1,3,16,128]{3,2,1,0:T(8,128)S(1)}, f32[1,3,16,128]{3,2,1,0:T(8,128)S(1)}, u32[]{:S(2)}, u32[]{:S(2)}) collective-permute-start(f32[1,3,16,128]{3,2,1,0:T(8,128)S(1)} %get-tuple-element.25), channel_id=1, source_target_pairs={{0,1},{1,2},{2,3},{3,0},{4,5},{5,6},{6,7},{7,4},{8,9},{9,10},{10,1... | collective-permute-start | bytes 73736 | tf_op jit(solution)/shard_map/ppermute | solution.py:786

commit v4 on v2

--- a/solution.py
+++ b/solution.py
@@ -226,7 +226,7 @@
         for shift in range(together):
             cell = index * together + shift
             spread_rows(position, params, cell, rows_ref, size_ref)
-            for first in range(0, EARLY_ROWS, SPAN):
+            for first in range(0, lanes, SPAN):
                 meet(cell, first, [(cell, 0.0, 0.0)], refs + (None, back_ref))
         return carry
 
@@ -249,10 +249,6 @@
             firsts = [part * SPAN for part in range(parts)]
 
             def all_rows(_, carry, firsts=firsts):
-                for first in firsts:
-                    if first >= EARLY_ROWS:
-                        meet(cell, first, [(cell, 0.0, 0.0)], refs + (None, back_ref))
-
                 def single(entry, carry):
                     for first in firsts:
                         meet(cell, first, [entry_of(entry)], refs + (total_ref, back_ref))

time: 121 us -> 120 us (level)
  blocking collectives: 34.9 us -> 28.2 us
  Pallas kernels: 66.5 us -> 72.3 us
    all_to_all x1, blocking collectives: 18.8 us -> 12.3 us  [shards(): lax.all_to_all(partial.reshape(holders, held * rows, lanes), 'bead', spli...]
    pallas_call x6, Pallas kernels: 66.5 us -> 72.3 us  [call(): pl.pallas_call(kernel, out_shape=outputs, in_specs=[pl.BlockSpec(memory_s...]
  transfers between devices with their start and end apart: 5 -> 5, of which waited for: 3 -> 3; matrix products, arithmetic and copies ran while one was open for 1% -> 1% of each run, Pallas kernels for 17% -> 18%
where the time goes in v4:
time: 120 us
  Pallas kernels  72.3 us (60%)
  blocking collectives  28.2 us (24%)
  waiting for transfers between devices  9.19 us (8%)
  starting transfers between devices  6.04 us (5%)
  other arithmetic  2.38 us (2%)
  local copies, waits for them, and re-layouts  1.58 us (1%)
    pallas_call x6, Pallas kernels, call(): pl.pallas_call(kernel, out_shape=outputs, in_specs=[pl.BlockSpec(memory_s...  72.3 us
    all_to_all x1, blocking collectives, shards(): got = lax.all_to_all(sent, 'bead', split_axis=0, concat_axis=0, tiled=True)  15.8 us
    all_to_all x1, blocking collectives, shards(): lax.all_to_all(partial.reshape(holders, held * rows, lanes), 'bead', spli...  12.3 us
    ppermute x1, waiting for transfers between devices, shards(): back = lax.ppermute(back, 'space', one_on)  4.43 us
    all_to_all x1, starting transfers between devices, shards(): lax.all_to_all(pieces, 'bead', split_axis=0, concat_axis=0, tiled=True)  3.43 us
    ppermute x1, waiting for transfers between devices, shards(): slow = slow + lax.ppermute(slow_back, 'space', one_on)  3.24 us
    ppermute x1, starting transfers between devices, shards(): next_stacked = lax.ppermute(stacked, 'space', one_back)  2.46 us
  transfers between devices with their start and end apart: 5, of which 3 were waited for; matrix products, arithmetic and copies ran while one was open for 1% of the time, Pallas kernels for 18%

profile of v4, /device:TPU:0, one launch (start us, length us, event | category | flops | bytes accessed | tf_op | source)
XLA Modules:
  0.0 120.5 jit_solution(6066170919030486834)
XLA Ops:
  0.6 0.0 copy-start
  0.6 0.8 select_reduce_fusion.2
  1.5 0.7 bitcast_select_fusion
  2.2 0.0 copy-done
  2.2 0.0 copy-start.5
  2.2 2.5 %collective-permute-start = (f32[5,3,16,128]{3,2,1,0:T(8,128)S(1)}, f32[5,3,16,128]{3,2,1,0:T(8,128)S(1)}, u32[]{:S(2)}, u32[]{:S(2)}) collective-permute-start(f32[5,3,16,128]{3,2,1,0:T(8,128)S(1)} %pad_maximum_fusion.1), channel_id=1, source_target_pairs={{1,0},{2,1},{3,2},{0,3},{5,4},{6,5},{7,6},{4,7},{9,8},{10,9},{11,1... | collective-permute-start | bytes 368648 | tf_op jit(solution)/shard_map/ppermute | solution.py:731
  4.7 0.0 copy-done.5
  4.7 0.1 iota_compare_fusion.2
  4.8 0.7 convert_reduce_fusion
  5.5 0.0 copy-start.8
  5.5 0.1 copy.24
  5.6 0.0 copy-start.7
  5.6 0.0 copy-start.3
  5.6 0.1 reshape.133
  5.7 0.4 copy-done.8
  6.2 0.1 copy-done.7
  6.3 0.0 copy-start.4
  6.3 0.1 concatenate.9.plan
  6.4 0.0 copy-done.3
  6.4 0.6 copy-done.4
  7.0 2.3 %shard_map.140 = (f32[4,16,8,128]{3,2,1,0:T(8,128)S(1)}, f32[8,128]{1,0:T(8,128)S(1)}, f32[64,96]{1,0:T(8,128)S(1)}) custom-call(f32[4,3,16,128]{3,2,1,0:T(8,128)S(1)} %bitcast.61, f32[3,16,128]{2,1,0:T(8,128)S(1)} %get-tuple-element.34.params, f32[8,128]{1,0:T(8,128)S(1)} %copy-done.4, f32[64,96]{1,0:T(8,128)S(1)} %copy-done.3), custom_call_target="tpu_custom_call" | custom-call | flops 4194304 | bytes 262144 | tf_op jit(solution)/shard_map/pallas_call | solution.py:566
  9.2 0.0 collective-permute-done
  9.3 0.0 copy-start.1
  9.3 0.0 copy-start.2
  9.3 47.4 %shard_map.141 = (f32[4,3,16,128]{3,2,1,0:T(8,128)S(1)}, f32[4,3,16,128]{3,2,1,0:T(8,128)S(1)}) custom-call(s32[1405]{0:T(1024)S(1)} %concatenate.9.plan, f32[4,3,16,128]{3,2,1,0:T(8,128)S(1)} %bitcast.62, f32[3,16,128]{2,1,0:T(8,128)S(1)} %get-tuple-element.34.params, f32[4,3,16,128]{3,2,1,0:T(8,128)S(1)} %slice.31.next_position, ...), custom_call_target="tpu_custom_call" | custom-call | flops 183500800 | bytes 262144 | tf_op jit(solution)/shard_map/pallas_call | solution.py:566
  56.7 0.1 collective-permute-start.1
  56.8 4.4 %collective-permute-done.1 = f32[4,3,16,128]{3,2,1,0:T(8,128)S(1)} collective-permute-done((f32[4,3,16,128]{3,2,1,0:T(8,128)S(1)}, f32[4,3,16,128]{3,2,1,0:T(8,128)S(1)}, u32[]{:S(2)}, u32[]{:S(2)}) %collective-permute-start.1) | collective-permute-done | bytes 98336 | tf_op jit(solution)/shard_map/ppermute | solution.py:756
  61.2 0.0 copy-done.1
  61.2 0.0 copy-done.2
  61.2 1.4 %shard_map.142 = (f32[8,48,128]{2,1,0:T(8,128)S(1)}, f32[8,72,128]{2,1,0:T(8,128)}) custom-call(s32[1]{0:T(128)} %bitcast.rank, f32[8,128]{1,0:T(8,128)S(1)} %get-tuple-element.15.table_hbm, f32[4,48,128]{2,1,0:T(8,128)S(1)} %bitcast.63, f32[4,48,128]{2,1,0:T(8,128)S(1)} %bitcast.64, f32[4,48,128]{2,1,0:T(8,128)S(1)} %bitcast.65, ...), custom_call_target="tpu_custom_call" | custom-call | flops 4194304 | bytes 262144 | tf_op jit(solution)/shard_map/pallas_call | solution.py:566
  62.7 12.3 %all_to_all.15 = f32[8,48,128]{2,1,0:T(8,128)S(1)} all-to-all(f32[8,48,128]{2,1,0:T(8,128)S(1)} %get-tuple-element.20), channel_id=1, replica_groups=mesh['bead'=8,'space'=4] {'bead'}, dimensions={0} | all-to-all | bytes 393216 | tf_op jit(solution)/shard_map/all_to_all | solution.py:779
  75.0 0.0 copy-start.6
  75.0 3.4 %all-to-all-start.1 = ((f32[8,72,128]{2,1,0:T(8,128)}), f32[8,72,128]{2,1,0:T(8,128)S(1)}, u32[]{:S(2)}, u32[]{:S(2)}) async-start(f32[8,72,128]{2,1,0:T(8,128)} %get-tuple-element.22), calls=%async_computation.1 | async-start | bytes 589824 | tf_op jit(solution)/shard_map/all_to_all | solution.py:785
  78.5 0.1 collective-permute-start.2
  78.6 1.5 %collective-permute-done.2.next_position = f32[1,3,16,128]{3,2,1,0:T(8,128)S(1)} collective-permute-done((f32[1,3,16,128]{3,2,1,0:T(8,128)S(1)}, f32[1,3,16,128]{3,2,1,0:T(8,128)S(1)}, u32[]{:S(2)}, u32[]{:S(2)}) %collective-permute-start.2) | collective-permute-done | bytes 24608 | tf_op jit(solution)/shard_map/ppermute | solution.py:784
  80.1 0.0 copy-done.6
  80.1 19.4 %shard_map.144 = (f32[1,3,16,128]{3,2,1,0:T(8,128)S(1)}, f32[1,3,16,128]{3,2,1,0:T(8,128)S(1)}) custom-call(s32[443]{0:T(512)S(1)} %copy-done.6, s32[16]{0:T(128)S(1)} %copy-done.5, f32[1,3,16,128]{3,2,1,0:T(8,128)S(1)} %bitcast.69, f32[3,16,128]{2,1,0:T(8,128)S(1)} %get-tuple-element.34.params, f32[1,3,16,128]{3,2,1,0:T(8,128)S(1)} %collective-permute-done.2.next_position, ...), custom_call_target="tpu_custom_call" | custom-call | flops 103546880 | bytes 262144 | tf_op jit(solution)/shard_map/pallas_call | solution.py:566
  99.5 0.0 collective-permute-start.3
  99.5 3.2 %collective-permute-done.3 = f32[1,3,16,128]{3,2,1,0:T(8,128)S(1)} collective-permute-done((f32[1,3,16,128]{3,2,1,0:T(8,128)S(1)}, f32[1,3,16,128]{3,2,1,0:T(8,128)S(1)}, u32[]{:S(2)}, u32[]{:S(2)}) %collective-permute-start.3) | collective-permute-done | bytes 24608 | tf_op jit(solution)/shard_map/ppermute | solution.py:789
  102.7 0.0 all-to-all-done.1.arrived
  102.7 0.5 shard_map.143
  103.3 15.8 %all_to_all.16 = f32[8,96,128]{2,1,0:T(8,128)S(1)} all-to-all(f32[8,96,128]{2,1,0:T(8,128)S(1)} %pad_maximum_fusion), channel_id=1, replica_groups=mesh['bead'=8,'space'=4] {'bead'}, dimensions={0} | all-to-all | bytes 786432 | tf_op jit(solution)/shard_map/all_to_all | solution.py:811
  119.1 1.3 %shard_map.145 = (f32[4,48,128]{2,1,0:T(8,128)}, f32[4,48,128]{2,1,0:T(8,128)}) custom-call(s32[1]{0:T(128)} %bitcast.rank, f32[8,128]{1,0:T(8,128)S(1)} %get-tuple-element.15.table_hbm, f32[8,48,128]{2,1,0:T(8,128)S(1)} %get-tuple-element.32.moved, f32[8,48,128]{2,1,0:T(8,128)S(1)} %get-tuple-element.31.slow, f32[3,16,128]{2,1,0:T(8,128)S(1)} %get-tuple-element.34.params), custom_call_target="tpu_custom_call" | custom-call | flops 1048576 | bytes 262144 | tf_op jit(solution)/shard_map/pallas_call | solution.py:566
  (11 shorter events, 0.2 us)
Async XLA Ops:
  0.6 1.6 %copy-start = (f32[4,16,3,128]{3,1,2,0:T(8,128)S(1)}, f32[4,16,3,128]{3,1,2,0:T(8,128)}, u32[]{:S(2)}) copy-start(f32[4,16,3,128]{3,1,2,0:T(8,128)} %param.13) | copy-start | bytes 294916
  2.2 2.5 %copy-start.5 = (s32[16]{0:T(128)S(1)}, s32[16]{0:T(128)}, u32[]{:S(2)}) copy-start(s32[16]{0:T(128)} %occupied.1) | copy-start | bytes 196
  2.2 7.0 %collective-permute-start = (f32[5,3,16,128]{3,2,1,0:T(8,128)S(1)}, f32[5,3,16,128]{3,2,1,0:T(8,128)S(1)}, u32[]{:S(2)}, u32[]{:S(2)}) collective-permute-start(f32[5,3,16,128]{3,2,1,0:T(8,128)S(1)} %pad_maximum_fusion.1), channel_id=1, source_target_pairs={{1,0},{2,1},{3,2},{0,3},{5,4},{6,5},{7,6},{4,7},{9,8},{10,9},{11,1... | collective-permute-start | bytes 368648 | tf_op jit(solution)/shard_map/ppermute | solution.py:731
  5.5 0.7 copy-start.8
  5.6 0.7 copy-start.7
  5.6 0.8 copy-start.3
  6.3 0.7 copy-start.4
  9.3 51.9 %copy-start.1 = (f32[4,16,3,128]{3,1,2,0:T(8,128)S(1)}, f32[4,16,3,128]{3,1,2,0:T(8,128)}, u32[]{:S(2)}) copy-start(f32[4,16,3,128]{3,1,2,0:T(8,128)} %param.14) | copy-start | bytes 294916
  9.3 51.9 %copy-start.2 = (f32[4,16,3,128]{3,1,2,0:T(8,128)S(1)}, f32[4,16,3,128]{3,1,2,0:T(8,128)}, u32[]{:S(2)}) copy-start(f32[4,16,3,128]{3,1,2,0:T(8,128)} %param.15) | copy-start | bytes 294916
  56.7 4.5 %collective-permute-start.1 = (f32[4,3,16,128]{3,2,1,0:T(8,128)S(1)}, f32[4,3,16,128]{3,2,1,0:T(8,128)S(1)}, u32[]{:S(2)}, u32[]{:S(2)}) collective-permute-start(f32[4,3,16,128]{3,2,1,0:T(8,128)S(1)} %get-tuple-element.19), channel_id=1, source_target_pairs={{0,1},{1,2},{2,3},{3,0},{4,5},{5,6},{6,7},{7,4},{8,9},{9,10},{10,1... | collective-permute-start | bytes 294920 | tf_op jit(solution)/shard_map/ppermute | solution.py:756
  75.0 5.0 %copy-start.6 = (s32[443]{0:T(512)S(1)}, s32[443]{0:T(512)}, u32[]{:S(2)}) copy-start(s32[443]{0:T(512)} %constant.35.clone.plan) | copy-start | bytes 5320
  75.0 27.7 %all-to-all-start.1 = ((f32[8,72,128]{2,1,0:T(8,128)}), f32[8,72,128]{2,1,0:T(8,128)S(1)}, u32[]{:S(2)}, u32[]{:S(2)}) async-start(f32[8,72,128]{2,1,0:T(8,128)} %get-tuple-element.22), calls=%async_computation.1 | async-start | bytes 589824 | tf_op jit(solution)/shard_map/all_to_all | solution.py:785
  78.5 1.6 %collective-permute-start.2 = (f32[1,3,16,128]{3,2,1,0:T(8,128)S(1)}, f32[1,3,16,128]{3,2,1,0:T(8,128)S(1)}, u32[]{:S(2)}, u32[]{:S(2)}) collective-permute-start(f32[1,3,16,128]{3,2,1,0:T(8,128)S(1)} %bitcast.68), channel_id=1, source_target_pairs={{1,0},{2,1},{3,2},{0,3},{5,4},{6,5},{7,6},{4,7},{9,8},{10,9},{11,1... | collective-permute-start | bytes 73736 | tf_op jit(solution)/shard_map/ppermute | solution.py:784
  99.5 3.3 %collective-permute-start.3 = (f32[1,3,16,128]{3,2,1,0:T(8,128)S(1)}, f32[1,3,16,128]{3,2,1,0:T(8,128)S(1)}, u32[]{:S(2)}, u32[]{:S(2)}) collective-permute-start(f32[1,3,16,128]{3,2,1,0:T(8,128)S(1)} %get-tuple-element.25), channel_id=1, source_target_pairs={{0,1},{1,2},{2,3},{3,0},{4,5},{5,6},{6,7},{7,4},{8,9},{9,10},{10,1... | collective-permute-start | bytes 73736 | tf_op jit(solution)/shard_map/ppermute | solution.py:789
